TPU v7x, 256 devices: a whole 4x4x8 slice. The times are simulated.
256 devices in a mesh: lon: 16 (over z, x_hi), lat: 16 (over x_lo, y, core).
Axes of the slice: x: 4 (x_hi: 2, x_lo: 2; x = x_hi * 2 + x_lo), y: 4, z: 8, core: 2. Of those that a mesh axis runs over, the one named last changes fastest.
Arguments:
- inputs: bfloat16 [2, 96, 192, 512], P(None, 'lat', 'lon'), may hold values from -6 to 6
- cotangent: bfloat16 [2, 96, 192, 512], P(None, 'lat', 'lon'), may hold values from -6 to 6
- pad_mask: int32 [96, 192], P('lat', 'lon'), may hold values 0 or 1
- rel_index: int32 [144, 144], replicated, may hold values from 0 to 758
- bias_table: float32 [759, 16], replicated, may hold values from -4 to 4
- ln_gain: float32 [512], replicated, may hold values from 0.1 to 1.9
- w_qkv: bfloat16 [512, 1536], replicated, may hold values from -4 to 4
- w_out: bfloat16 [512, 512], replicated, may hold values from -0.25 to 0.25
Outputs:
- grad_inputs: float32 [2, 96, 192, 512], P(None, 'lat', 'lon')
- grad_gain: float32 [512], replicated
- grad_wqkv: float32 [512, 1536], replicated
- grad_wout: float32 [512, 512], replicated
- grad_table: float32 [759, 16], replicated
All inputs are finite; a program needn't handle non-finite values. No bound on the sum of `pad_mask` on one device may be relied on, other than what follows from the above.
Results may differ from a plain program's by a relative error of at most 0.0095.
The roundings to bfloat16 on the way count: a program that leaves them out, or rounds other values in their place, can miss the bound.
Values may be sent and summed in bfloat16 or wider, within the bound.
A program may use at most 64 MiB of HBM per device.

v0:
```python
import jax
import jax.numpy as jnp
from jax import lax
from jax.sharding import PartitionSpec as P

WLEV = 2
WLAT = 6
WLON = 12


EPSILON = 1e-05
MASKED = -30000.0


def shifted_2(x, axis, by):
    size = lax.axis_size(axis)
    return lax.ppermute(x, axis, [(i, (i + by) % size) for i in range(size)])


def to_windows(array_in):
    lev_count, row_count, col_count, feat_count = array_in.shape
    pieces = array_in.reshape(
        lev_count // WLEV, WLEV, row_count // WLAT, WLAT, col_count // WLON, WLON, feat_count
    )
    pieces = pieces.transpose(0, 2, 4, 1, 3, 5, 6)
    return pieces.reshape(-1, WLEV * WLAT * WLON, feat_count)


def from_windows(array_in, lev_count, row_count, col_count):
    feat_count = array_in.shape[-1]
    pieces = array_in.reshape(
        lev_count // WLEV, row_count // WLAT, col_count // WLON, WLEV, WLAT, WLON, feat_count
    )
    pieces = pieces.transpose(0, 3, 1, 4, 2, 5, 6)
    return pieces.reshape(lev_count, row_count, col_count, feat_count)


def pair_blocks(rel_index):
    window_size = rel_index.shape[0]
    return rel_index.reshape(-1, 8 * window_size)


def table_lookup(rel_index, bias_table):
    window_size = rel_index.shape[0]
    entries = jnp.arange(bias_table.shape[0], dtype=jnp.int32)

    def lookup_block(index_block):
        one_hot = (index_block[:, None] == entries[None, :]).astype(jnp.float32)
        return jnp.dot(one_hot, bias_table, precision=lax.Precision.HIGHEST)

    looked = lax.map(lookup_block, pair_blocks(rel_index))
    return looked.reshape(window_size, window_size, bias_table.shape[1])


def table_scatter(rel_index, pair_sums, entry_count):
    entries = jnp.arange(entry_count, dtype=jnp.int32)
    index_blocks = pair_blocks(rel_index)
    sum_blocks = pair_sums.reshape(index_blocks.shape[0], index_blocks.shape[1], pair_sums.shape[1])

    def scatter_block(total, block_in):
        one_hot = (block_in[0][:, None] == entries[None, :]).astype(jnp.float32)
        term = lax.dot_general(
            one_hot, block_in[1], (((0,), (0,)), ((), ())), precision=lax.Precision.HIGHEST
        )
        return (total + term, None)

    start = jnp.zeros((entry_count, pair_sums.shape[1]), jnp.float32)
    total, unused = lax.scan(scatter_block, start, (index_blocks, sum_blocks))
    return total


def window_grads(
    inputs, cotangent, valid_keys, group_ids, rel_index, bias_table, ln_gain, w_qkv, w_out
):
    lev_count, row_count, col_count, feat_count = inputs.shape
    head_count = bias_table.shape[1]
    head_size = feat_count // head_count
    score_scale = head_size ** (-0.5)
    f32 = jnp.float32
    values_f = inputs.astype(f32)
    center = values_f - jnp.mean(values_f, axis=-1, keepdims=True)
    variance = jnp.mean(center * center, axis=-1, keepdims=True)
    inv_std = lax.rsqrt(variance + EPSILON)
    standard = center * inv_std
    normed = (standard * ln_gain).astype(jnp.bfloat16)
    window_in = to_windows(normed)
    window_count, window_size = (window_in.shape[0], window_in.shape[1])
    tokens_in = window_in.reshape(-1, feat_count)
    flat_cot = to_windows(cotangent).reshape(-1, feat_count)
    key_valid = to_windows(
        jnp.broadcast_to(valid_keys[None, :, :, None], (lev_count, row_count, col_count, 1))
    )[..., 0]
    key_group = to_windows(
        jnp.broadcast_to(group_ids[None, :, :, None], (lev_count, row_count, col_count, 1))
    )[..., 0]
    projected = jnp.dot(tokens_in, w_qkv, preferred_element_type=f32)
    shape_heads = (window_count, window_size, head_count, head_size)
    query_heads = projected[:, :feat_count].astype(jnp.bfloat16).reshape(shape_heads)
    key_heads = projected[:, feat_count : 2 * feat_count].astype(jnp.bfloat16).reshape(shape_heads)
    value_heads = projected[:, 2 * feat_count :].astype(jnp.bfloat16).reshape(shape_heads)
    bias_pairs = table_lookup(rel_index, bias_table).transpose(2, 0, 1)
    same_group = key_group[:, :, None] == key_group[:, None, :]
    key_seen = (key_valid[:, None, :] > 0.5) | jnp.eye(window_size, dtype=bool)[None]
    allowed = (same_group & key_seen)[:, None]
    scores = (
        jnp.einsum("nqhd,nkhd->nhqk", query_heads, key_heads, preferred_element_type=f32)
        * score_scale
    )
    scores = jnp.where(allowed, scores + bias_pairs[None], MASKED)
    row_max = jnp.max(scores, axis=-1, keepdims=True)
    exponent = jnp.exp(scores - row_max)
    attn_probs = exponent / jnp.sum(exponent, axis=-1, keepdims=True)
    probs_b = attn_probs.astype(jnp.bfloat16)
    attended = jnp.einsum("nhqk,nkhd->nqhd", probs_b, value_heads, preferred_element_type=f32)
    attended = attended.astype(jnp.bfloat16).reshape(-1, feat_count)
    grad_wout = lax.dot_general(
        attended, flat_cot, (((0,), (0,)), ((), ())), preferred_element_type=f32
    )
    grad_att = lax.dot_general(
        flat_cot, w_out, (((1,), (1,)), ((), ())), preferred_element_type=f32
    )
    grad_att = grad_att.astype(jnp.bfloat16).reshape(shape_heads)
    grad_probs = jnp.einsum("nqhd,nkhd->nhqk", grad_att, value_heads, preferred_element_type=f32)
    grad_values = jnp.einsum(
        "nhqk,nqhd->nkhd", probs_b, grad_att, preferred_element_type=f32
    ).astype(jnp.bfloat16)
    grad_scores = attn_probs * (
        grad_probs - jnp.sum(attn_probs * grad_probs, axis=-1, keepdims=True)
    )
    pair_sums = jnp.sum(grad_scores, axis=0).transpose(1, 2, 0).reshape(-1, head_count)
    grad_table = table_scatter(rel_index, pair_sums, bias_table.shape[0])
    scores_b = grad_scores.astype(jnp.bfloat16)
    grad_query = (
        jnp.einsum("nhqk,nkhd->nqhd", scores_b, key_heads, preferred_element_type=f32) * score_scale
    ).astype(jnp.bfloat16)
    grad_keys = (
        jnp.einsum("nhqk,nqhd->nkhd", scores_b, query_heads, preferred_element_type=f32)
        * score_scale
    ).astype(jnp.bfloat16)
    grad_proj = jnp.concatenate(
        [
            grad_query.reshape(-1, feat_count),
            grad_keys.reshape(-1, feat_count),
            grad_values.reshape(-1, feat_count),
        ],
        axis=1,
    )
    grad_wqkv = lax.dot_general(
        tokens_in, grad_proj, (((0,), (0,)), ((), ())), preferred_element_type=f32
    )
    grad_normed = lax.dot_general(
        grad_proj, w_qkv, (((1,), (1,)), ((), ())), preferred_element_type=f32
    )
    grad_normed = from_windows(
        grad_normed.reshape(window_count, window_size, feat_count), lev_count, row_count, col_count
    )
    grad_gain = jnp.sum(grad_normed * standard, axis=(0, 1, 2))
    grad_hat = grad_normed * ln_gain
    grad_in = inv_std * (
        grad_hat
        - jnp.mean(grad_hat, axis=-1, keepdims=True)
        - standard * jnp.mean(grad_hat * standard, axis=-1, keepdims=True)
    )
    return (grad_in, (grad_gain, grad_wqkv, grad_wout, grad_table))


def lon_roll(fields):
    half_span = WLON // 2
    values_in, cot_in, valid_in = fields
    arrived = shifted_2(
        (values_in[:, :, :half_span], cot_in[:, :, :half_span], valid_in[:, :half_span]), "lon", -1
    )
    return (
        jnp.concatenate([values_in[:, :, half_span:], arrived[0]], axis=2),
        jnp.concatenate([cot_in[:, :, half_span:], arrived[1]], axis=2),
        jnp.concatenate([valid_in[:, half_span:], arrived[2]], axis=1),
    )


def lat_roll(fields):
    half_span = WLAT // 2
    values_in, cot_in, valid_in = fields
    arrived = shifted_2(
        (values_in[:, :half_span], cot_in[:, :half_span], valid_in[:half_span]), "lat", -1
    )
    return (
        jnp.concatenate([values_in[:, half_span:], arrived[0]], axis=1),
        jnp.concatenate([cot_in[:, half_span:], arrived[1]], axis=1),
        jnp.concatenate([valid_in[half_span:], arrived[2]], axis=0),
    )


def lon_back(grad_field):
    half_span = WLON // 2
    arrived = shifted_2(grad_field[:, :, -half_span:], "lon", 1)
    return jnp.concatenate([arrived, grad_field[:, :, :-half_span]], axis=2)


def lat_back(grad_field):
    half_span = WLAT // 2
    arrived = shifted_2(grad_field[:, -half_span:], "lat", 1)
    return jnp.concatenate([arrived, grad_field[:, :-half_span]], axis=1)


def per_device(inputs, cotangent, pad_mask, rel_index, bias_table, ln_gain, w_qkv, w_out):
    lev_count, row_count, col_count, feat_count = inputs.shape
    fields = (inputs, cotangent, pad_mask.astype(jnp.bfloat16))
    fields = lat_roll(lon_roll(fields))
    shifted, shifted_cot, shifted_pad = fields
    lat_total = row_count * lax.axis_size("lat")
    row_global = lax.axis_index("lat") * row_count + jnp.arange(row_count, dtype=jnp.int32)
    group_rows = (row_global >= lat_total - WLAT // 2).astype(jnp.int32)
    group_ids = jnp.broadcast_to(group_rows[:, None], (row_count, col_count))
    grad_shifted, grad_parts = window_grads(
        shifted,
        shifted_cot,
        shifted_pad.astype(jnp.float32),
        group_ids,
        rel_index,
        bias_table,
        ln_gain,
        w_qkv,
        w_out,
    )
    grad_inputs = lon_back(lat_back(grad_shifted))
    totals = lax.psum((grad_parts[0], grad_parts[1], grad_parts[2], grad_parts[3]), ("lon", "lat"))
    token_total = lev_count * lat_total * col_count * lax.axis_size("lon")
    grad_scale = float(token_total) ** (-0.5)
    return (
        grad_inputs,
        totals[0] * grad_scale,
        totals[1] * grad_scale,
        totals[2] * grad_scale,
        totals[3] * grad_scale,
    )


def solution(mesh):
    in_specs = (
        P(None, "lat", "lon", None),
        P(None, "lat", "lon", None),
        P("lat", "lon"),
        P(),
        P(),
        P(),
        P(),
        P(),
    )
    out_specs = (P(None, "lat", "lon", None), P(), P(), P(), P())
    return jax.shard_map(
        per_device, mesh=mesh, in_specs=in_specs, out_specs=out_specs, check_vma=False
    )
```

profile of v0, /device:TPU:1, one launch (start us, length us, event | category | flops | bytes accessed | tf_op | source)
XLA Modules:
  0.0 422.6 jit_solution(4645623373827279512)
XLA Ops:
  7.2 1.1 fusion.39
  9.0 8.9 %collective-permute-start = (bf16[2,6,6,512]{3,2,1,0:T(8,128)(2,1)}, bf16[2,6,6,512]{3,2,1,0:T(8,128)(2,1)}, u32[]{:S(2)}, u32[]{:S(2)}) collective-permute-start(bf16[2,6,6,512]{3,2,1,0:T(8,128)(2,1)} %copy.52), channel_id=1, source_target_pairs={{0,240},{16,0},{32,16},{48,32},{64,48},{80,64},{96,80},{112,96},{1... | collective-permute-start | bytes 221192 | tf_op jit(solution)/shard_map/ppermute | solution.py:17
  17.9 1.7 fusion.40
  20.6 3.2 collective-permute-start.2
  23.8 1.7 reshape.285
  25.4 71.2 %while.22 = (s32[]{:T(128)}, f32[18,1152,16]{1,0,2:T(8,128)S(1)}, s32[18,1152]{1,0:T(8,128)}, f32[759,16]{0,1:T(8,128)}, s32[]{:T(128)}, /*index=5*/s32[]{:T(128)}) while((s32[]{:T(128)}, f32[18,1152,16]{1,0,2:T(8,128)S(1)}, s32[18,1152]{1,0:T(8,128)}, f32[759,16]{0,1:T(8,128)}, s32[]{:T(128)}, /*index=5*/s32[]{:T(128)}) %tuple.60), condition=%wide.region_3.4_spmd.clone, body=%wide.region_2.3_spmd.clone.sunk | while | flops 168753024 | bytes 431125 | solution.py:51
  26.2 2.5 fusion.65
  30.2 2.5 fusion.65
  34.1 2.5 fusion.65
  38.1 2.5 fusion.65
  42.0 2.5 fusion.65
  46.0 2.5 fusion.65
  50.0 2.5 fusion.65
  53.9 2.5 fusion.65
  57.9 2.5 fusion.65
  61.8 2.5 fusion.65
  65.8 2.5 fusion.65
  69.7 2.5 fusion.65
  73.7 2.5 fusion.65
  77.7 2.5 fusion.65
  81.6 2.5 fusion.65
  85.6 2.5 fusion.65
  89.5 2.5 fusion.65
  93.5 2.5 fusion.65
  96.6 2.9 reshape.286
  99.5 3.5 copy.32
  103.1 1.5 collective-permute-start.3
  104.8 2.3 collective-permute-done.3
  109.8 4.1 collective-permute-start.5
  117.9 3.7 fusion.35
  126.5 1.4 multiply_reduce_fusion.2
  127.9 2.4 fusion.23
  130.3 1.3 convolution_convert_fusion.1
  132.7 5.4 %fusion.10 = f32[144,144,16]{0,1,2:T(8,128)} fusion(f32[16,144,144]{1,2,0:T(8,128)} %copy-done.1, f32[144,144,16]{0,1,2:T(8,128)} %copy.32, f32[16,144,144]{1,2,0:T(8,128)} %get-tuple-element.139, f32[144,16]{0,1:T(8,128)S(1)} %bitcast.97, f32[144,16]{0,1:T(8,128)S(1)} %bitcast.96, f32[144,16]{0,1:T(8,128)S(1)} %bitcast.88, pred[144,144]{0,1:T(8,128)(4,1)S(1)} %fusion.27), kind=kLoop, calls=%fused_computation.16 | loop fusion | flops 2322432 | bytes 5356800 | tf_op jit(solution)/shard_map/mul | solution.py:127
  138.1 3.5 copy.41
  141.6 2.6 reshape_reshape.3
  144.1 2.2 fusion.43
  147.1 36.3 %while.23 = (s32[]{:T(128)}, f32[759,16]{0,1:T(8,128)S(1)}, s32[18,1152]{1,0:T(8,128)}, f32[18,1152,16]{1,0,2:T(8,128)S(1)}, s32[]{:T(128)}, /*index=5*/s32[]{:T(128)}) while((s32[]{:T(128)}, f32[759,16]{0,1:T(8,128)S(1)}, s32[18,1152]{1,0:T(8,128)}, f32[18,1152,16]{1,0,2:T(8,128)S(1)}, s32[]{:T(128)}, ...), condition=%wide.region_14.15_spmd.clone, body=%wide.region_13.14_spmd.clone.sunk | while | flops 168777312 | bytes 332255 | solution.py:68
  148.0 1.1 fusion.66
  150.0 1.1 fusion.66
  152.0 1.1 fusion.66
  154.1 1.1 fusion.66
  156.1 1.1 fusion.66
  158.1 1.1 fusion.66
  160.1 1.1 fusion.66
  162.1 1.1 fusion.66
  164.1 1.1 fusion.66
  166.2 1.1 fusion.66
  168.2 1.1 fusion.66
  170.2 1.1 fusion.66
  172.2 1.1 fusion.66
  174.2 1.1 fusion.66
  176.2 1.1 fusion.66
  178.3 1.1 fusion.66
  180.3 1.1 fusion.66
  182.3 1.1 fusion.66
  183.4 77.0 %all-reduce = (f32[512]{0:T(512)S(1)}, f32[759,16]{0,1:T(8,128)S(1)}) all-reduce(f32[512]{0:T(512)S(1)} %get-tuple-element.97, f32[759,16]{0,1:T(8,128)S(1)} %get-tuple-element.60), channel_id=1, replica_groups=mesh['lon'=16,'lat'=16] {'lon','lat'}, use_global_device_ids=true, to_apply=%region_10.11 | all-reduce | flops 12656 | bytes 101248 | tf_op jit(solution)/shard_map/psum | solution.py:226
  261.1 1.1 fusion.25
  262.1 1.2 collective-permute-start.7
  263.9 7.6 %collective-permute-done.7 = f32[2,6,6,512]{3,2,1,0:T(8,128)S(1)} collective-permute-done((f32[2,6,6,512]{3,2,1,0:T(8,128)S(1)}, f32[2,6,6,512]{3,2,1,0:T(8,128)S(1)}, u32[]{:S(2)}, u32[]{:S(2)}) %collective-permute-start.7) | collective-permute-done | bytes 147488 | tf_op jit(solution)/shard_map/ppermute | solution.py:17
  271.4 1.1 fusion.22
  273.5 137.2 %all-reduce.4.cloned.1.call-done = (f32[512,1536]{1,0:T(8,128)}, f32[512,512]{1,0:T(8,128)}) async-done(((f32[512,1536]{1,0:T(8,128)}, f32[512,512]{1,0:T(8,128)}), (f32[512,1536]{1,0:T(8,128)}, f32[512,512]{1,0:T(8,128)})) %all-reduce.4.cloned.1.call-update) | async-done | bytes 4194320 | tf_op jit(solution)/shard_map/psum | solution.py:226
  410.7 4.0 broadcast_multiply_fusion
  414.7 1.1 broadcast_multiply_fusion.1
  (171 shorter events, 58.0 us)
Async XLA Ops:
  7.2 109.1 %copy-start = (bf16[512,1536]{1,0:T(8,128)(2,1)S(1)}, bf16[512,1536]{1,0:T(8,128)(2,1)}, u32[]{:S(2)}) copy-start(bf16[512,1536]{1,0:T(8,128)(2,1)} %param.18) | copy-start | bytes 4718596
  7.2 403.5 %all-reduce.4.cloned.1.call-start = ((), (), s32[]{:S(2)}) async-start(), calls=%async_computation | async-start | bytes 8388608 | tf_op jit(solution)/shard_map/psum | solution.py:226
  9.0 98.3 %collective-permute-start = (bf16[2,6,6,512]{3,2,1,0:T(8,128)(2,1)}, bf16[2,6,6,512]{3,2,1,0:T(8,128)(2,1)}, u32[]{:S(2)}, u32[]{:S(2)}) collective-permute-start(bf16[2,6,6,512]{3,2,1,0:T(8,128)(2,1)} %copy.52), channel_id=1, source_target_pairs={{0,240},{16,0},{32,16},{48,32},{64,48},{80,64},{96,80},{112,96},{1... | collective-permute-start | bytes 221192 | tf_op jit(solution)/shard_map/ppermute | solution.py:17
  19.6 89.3 %collective-permute-start.4 = (bf16[2,6,6,512]{3,0,2,1:T(2,128)(2,1)}, bf16[2,6,6,512]{3,0,2,1:T(2,128)(2,1)}, u32[]{:S(2)}, u32[]{:S(2)}) collective-permute-start(bf16[2,6,6,512]{3,0,2,1:T(2,128)(2,1)} %get-tuple-element.134), channel_id=1, source_target_pairs={{0,240},{16,0},{32,16},{48,32},{64,48},{80,64},{96,80},{112,96},{1... | collective-permute-start | bytes 221192 | tf_op jit(solution)/shard_map/ppermute | solution.py:17
  20.6 82.5 %collective-permute-start.2 = (bf16[6,6]{1,0:T(8,128)(2,1)S(1)}, bf16[6,6]{1,0:T(8,128)(2,1)S(1)}, u32[]{:S(2)}, u32[]{:S(2)}) collective-permute-start(bf16[6,6]{1,0:T(8,128)(2,1)S(1)} %get-tuple-element.138), channel_id=1, source_target_pairs={{0,240},{16,0},{32,16},{48,32},{64,48},{80,64},{96,80},{112,96},{1... | collective-permute-start | bytes 224 | tf_op jit(solution)/shard_map/ppermute | solution.py:17
  99.5 9.3 %copy-start.5 = (bf16[2,6,6,512]{3,0,2,1:T(2,128)(2,1)S(1)}, bf16[2,6,6,512]{3,0,2,1:T(2,128)(2,1)}, u32[]{:S(2)}) copy-start(bf16[2,6,6,512]{3,0,2,1:T(2,128)(2,1)} %get-tuple-element.133) | copy-start | bytes 221188
  103.0 12.0 %copy-start.3 = (bf16[512,512]{1,0:T(8,128)(2,1)S(1)}, bf16[512,512]{1,0:T(8,128)(2,1)}, u32[]{:S(2)}) copy-start(bf16[512,512]{1,0:T(8,128)(2,1)} %param.19) | copy-start | bytes 1572868
  103.1 4.0 collective-permute-start.3
  104.7 11.5 %copy-start.9 = (f32[512]{0:T(512)S(1)}, f32[512]{0:T(512)}, u32[]{:S(2)}) copy-start(f32[512]{0:T(512)} %param.17) | copy-start | bytes 6148
  108.2 5.6 %collective-permute-start.1 = (bf16[2,3,12,512]{3,2,1,0:T(8,128)(2,1)S(1)}, bf16[2,3,12,512]{3,2,1,0:T(8,128)(2,1)S(1)}, u32[]{:S(2)}, u32[]{:S(2)}) collective-permute-start(bf16[2,3,12,512]{3,2,1,0:T(8,128)(2,1)S(1)} %get-tuple-element.128), channel_id=1, source_target_pairs={{0,15},{1,0},{2,1},{3,2},{4,3},{5,4},{6,5},{7,6},{8,7},{9,8},{10,9... | collective-permute-start | bytes 221192 | tf_op jit(solution)/shard_map/ppermute | solution.py:17
  109.8 5.0 %collective-permute-start.5 = (bf16[2,3,12,512]{3,0,2,1:T(2,128)(2,1)S(1)}, bf16[2,3,12,512]{3,0,2,1:T(2,128)(2,1)S(1)}, u32[]{:S(2)}, u32[]{:S(2)}) collective-permute-start(bf16[2,3,12,512]{3,0,2,1:T(2,128)(2,1)S(1)} %get-tuple-element.132), channel_id=1, source_target_pairs={{0,15},{1,0},{2,1},{3,2},{4,3},{5,4},{6,5},{7,6},{8,7},{9,8},{10,9... | collective-permute-start | bytes 221192 | tf_op jit(solution)/shard_map/ppermute | solution.py:17
  121.6 0.9 copy-start.7
  122.5 0.9 copy-start.6
  124.3 1.4 copy-start.1
  130.3 1.3 copy-start.4
  132.7 128.3 %collective-permute-start.6 = (f32[2,3,12,512]{3,2,1,0:T(8,128)}, f32[2,3,12,512]{3,2,1,0:T(8,128)}, u32[]{:S(2)}, u32[]{:S(2)}) collective-permute-start(f32[2,3,12,512]{3,2,1,0:T(8,128)} %get-tuple-element.125), channel_id=1, source_target_pairs={{0,1},{1,2},{2,3},{3,4},{4,5},{5,6},{6,7},{7,8},{8,9},{9,10},{10,1... | collective-permute-start | bytes 442376 | tf_op jit(solution)/shard_map/ppermute | solution.py:17
  146.3 0.8 copy-start.8
  262.1 9.3 %collective-permute-start.7 = (f32[2,6,6,512]{3,2,1,0:T(8,128)S(1)}, f32[2,6,6,512]{3,2,1,0:T(8,128)S(1)}, u32[]{:S(2)}, u32[]{:S(2)}) collective-permute-start(f32[2,6,6,512]{3,2,1,0:T(8,128)S(1)} %fusion.25), channel_id=1, source_target_pairs={{0,16},{16,32},{32,48},{48,64},{64,80},{80,96},{96,112},{112,128},... | collective-permute-start | bytes 442376 | tf_op jit(solution)/shard_map/ppermute | solution.py:17
  410.7 4.0 copy-start.2
Sparse Core Ops, SparseCore 0:
  146.5 264.1 all-reduce.3
where the time goes:
time: 427 us; the launch traced here: 423 us
  waiting for transfers between devices  147 us (34%)
  matrix products  79.7 us (19%)
  blocking collectives  77 us (18%)
  local copies, waits for them, and re-layouts  65.2 us (15%)
  starting transfers between devices  19.7 us (5%)
  other arithmetic  18.3 us (4%)
  between operations  14.3 us (3%)
    psum x1, waiting for transfers between devices, per_device(): lax.psum((grad_parts[0], grad_parts[1], grad_parts[2], grad_parts[3]), ('...  137 us
    psum x1, blocking collectives, per_device(): lax.psum((grad_parts[0], grad_parts[1], grad_parts[2], grad_parts[3]), ('...  77 us
    dot_general x18, matrix products, lookup_block(): return jnp.dot(one_hot, bias_table, precision=lax.Precision.HIGHEST)  45.5 us
    dynamic_slice x36, local copies, waits for them, and re-layouts, table_lookup(): looked = lax.map(lookup_block, pair_blocks(rel_index))  28.6 us
    dot_general x18, matrix products, scatter_block(): lax.dot_general(one_hot, block_in[1], (((0,), (0,)), ((), ())), precision...  20.4 us
    ppermute x8, starting transfers between devices, shifted_2(): return lax.ppermute(x, axis, [(i, (i + by) % size) for i in range(size)])  19.6 us
    dynamic_update_slice x36, local copies, waits for them, and re-layouts, table_lookup(): looked = lax.map(lookup_block, pair_blocks(rel_index))  10.9 us
    ppermute x8, waiting for transfers between devices, shifted_2(): return lax.ppermute(x, axis, [(i, (i + by) % size) for i in range(size)])  10.2 us
  transfers between devices with their start and end apart: 9, of which 4 were waited for; matrix products, arithmetic and copies ran while one was open for 33% of the time, Pallas kernels for 0%

commit v1 on v0

v1 whole, which is shorter than its diff:
```python
import jax
import jax.numpy as jnp
from jax import lax
from jax.experimental import pallas as pl
from jax.experimental.pallas import tpu as pltpu
from jax.sharding import PartitionSpec as P

F32 = jnp.float32
BF16 = jnp.bfloat16
I32 = jnp.int32
MESH = pl.DeviceIdType.MESH

EPSILON = 1e-05
MASKED = -30000.0
WT = 144
FEAT = 512
HEADS = 16
HEAD_SIZE = 32
NBIAS = 759
SCORE_SCALE = HEAD_SIZE ** (-0.5)
GRAD_SCALE = 36864.0 ** (-0.5)

NN = (((1,), (0,)), ((), ()))
NT = (((1,), (1,)), ((), ()))

HALO = 0
CORE = 9
RS1 = 13
RS2 = 19
RS3 = 25
AG1 = 39
AG2 = 53
AG3 = 59
SIB = 65
TCORE = 73
TX = 74
TY = 77
TZ = 80
TXG = 87
TSIB = 90
BACK = 91
SEMS = 94


def mm(a, b, dims=NN):
    return lax.dot_general(a, b, dims, preferred_element_type=F32)


def iota(shape, dim):
    return lax.broadcasted_iota(I32, shape, dim)


def body(
    x_ref, cot_ref, pad_ref, rel_ref, bias_ref, gain_ref, wqkv_ref, wout_ref,
    big_ref, gin_ref, table_ref, ggain_ref,
    xw, cw, pads, padf, relt, tab, bias, allow, std, istd, nrm, nrmt, cotf,
    proj, projt, gatt, gattt, attt, gradt, ds,
    sib_send, sib_recv, own_half, pay, r1, s1, r2, s2, r3,
    tsum, tb, rt0, t1, rt1, t2, rt2, t3, rt3, tf,
    back_send, back_recv, ginf, ssem, rsem,
):
    lon = lax.axis_index("lon")
    lat = lax.axis_index("lat")
    z, xhi = lon // 2, lon % 2
    xlo, rest = lat // 8, lat % 8
    y, core = rest // 2, rest % 2
    x = xhi * 2 + xlo

    def at_x(value):
        return (z * 2 + value // 2, (value % 2) * 8 + rest)

    def at_y(value):
        return (lon, xlo * 8 + value * 2 + core)

    def at_z(value):
        return (value * 2 + xhi, lat)

    sibling = (lon, xlo * 8 + y * 2 + (1 - core))
    west, east = (lon + 15) % 16, (lon + 1) % 16
    south, north = (lat + 15) % 16, (lat + 1) % 16

    def copy(src, dst, index, device):
        made = pltpu.make_async_remote_copy(
            src_ref=src, dst_ref=dst, send_sem=ssem.at[index], recv_sem=rsem.at[index],
            device_id=device, device_id_type=MESH,
        )
        return made

    barrier = pltpu.get_barrier_semaphore()
    partners = [sibling, (west, lat), (lon, south), (west, south), (east, lat), (lon, north), (east, north)]
    partners += [at_x((x + d) % 4) for d in range(1, 4)]
    partners += [at_y((y + d) % 4) for d in range(1, 4)]
    partners += [at_z((z + d) % 8) for d in range(1, 8)]
    for device in partners:
        pl.semaphore_signal(barrier, inc=1, device_id=device, device_id_type=MESH)
    pl.semaphore_wait(barrier, len(partners))

    halo = []
    places = (
        ((3, 0), (0, 6), (west, lat)),
        ((0, 6), (3, 0), (lon, south)),
        ((0, 0), (3, 6), (west, south)),
    )
    for n, (source, target, device) in enumerate(places):
        for m, (field, window) in enumerate(((x_ref, xw), (cot_ref, cw))):
            halo.append(copy(
                field.at[pl.ds(source[0], 3), pl.ds(source[1], 6)],
                window.at[pl.ds(target[0], 3), pl.ds(target[1], 6)],
                HALO + 3 * n + m, device,
            ))
        halo.append(copy(pad_ref, pads.at[n], HALO + 3 * n + 2, device))
    for made in halo:
        made.start()
    pltpu.sync_copy(x_ref.at[pl.ds(3, 3), pl.ds(6, 6)], xw.at[pl.ds(0, 3), pl.ds(0, 6)])
    pltpu.sync_copy(cot_ref.at[pl.ds(3, 3), pl.ds(6, 6)], cw.at[pl.ds(0, 3), pl.ds(0, 6)])

    token = iota((WT, WT), 0)
    order = (iota((WT, WT), 1) == (token % 2) * 72 + token // 2).astype(BF16)
    rel = rel_ref[...]
    low = mm(mm(order, (rel & 255).astype(F32).astype(BF16), NT).astype(BF16), order, NT)
    high = mm(mm(order, (rel >> 8).astype(F32).astype(BF16), NT).astype(BF16), order, NT)
    relt[...] = jnp.zeros((WT, 256), I32)
    relt[:, :WT] = (high * 256.0 + low).astype(I32)
    tab[...] = jnp.zeros((HEADS, 1, 768), F32)
    for head in range(HEADS):
        tab[head, :, :NBIAS] = bias_ref[head:head + 1, :]

    def lookup(head, carry):
        for part in range(2):
            index = relt[:, 128 * part:128 * part + 128]
            lane, chunk = index & 127, index >> 7
            found = jnp.zeros((WT, 128), F32)
            for c in range(6):
                row = jnp.broadcast_to(tab[head, :, 128 * c:128 * c + 128], (WT, 128))
                taken = jnp.take_along_axis(row, lane, axis=1, mode="promise_in_bounds")
                found = jnp.where(chunk == c, taken, found)
            if part == 0:
                bias[head, :, 0:128] = found
            else:
                bias[head, :, 128:WT] = found[:, 0:WT - 128]
        return carry

    lax.fori_loop(0, HEADS, lookup, 0)

    for made in halo:
        made.wait_recv()

    padf[...] = jnp.zeros((32, 128), F32)
    padf[0:6, 0:12] = pad_ref[...].astype(F32)
    for n in range(3):
        padf[8 * n + 8:8 * n + 14, 0:12] = pads[n].astype(F32)

    def spot(token_at):
        row, col = token_at // 24, (token_at % 24) // 2
        slot = (row >= 3).astype(I32) * 2 + (col >= 6).astype(I32)
        return row, slot, row + jnp.where(row < 3, 3, -3), col + jnp.where(col < 6, 6, -6)

    row, slot, source_row, unused = spot(iota((WT, 32), 0))
    row_pick = (iota((WT, 32), 1) == slot * 8 + source_row).astype(BF16)
    unused, unused, unused, source_col = spot(iota((WT, 128), 0))
    picked = mm(row_pick, padf[...].astype(BF16))
    valid = jnp.sum(jnp.where(iota((WT, 128), 1) == source_col, picked, 0.0), axis=1, keepdims=True)
    key, query = iota((WT, WT), 0), iota((WT, WT), 1)
    same_group = ((key >= 72) == (query >= 72)) | (lat != 15)
    allow[...] = (same_group & ((valid > 0.5) | (key == query))).astype(F32)

    tokens = xw[...].astype(F32).reshape(WT, FEAT)
    center = tokens - jnp.mean(tokens, axis=-1, keepdims=True)
    variance = jnp.mean(center * center, axis=-1, keepdims=True)
    inv_std = lax.rsqrt(variance + EPSILON)
    standard = center * inv_std
    std[...] = standard
    istd[...] = inv_std
    normed = (standard * gain_ref[...]).astype(BF16)
    nrm[...] = normed
    nrmt[...] = normed.T
    cotf[...] = cw[...].reshape(WT, FEAT)
    proj[...] = mm(nrm[...], wqkv_ref[...]).astype(BF16)
    projt[...] = proj[...].T
    gatt[...] = mm(cotf[...], wout_ref[...], NT).astype(BF16)
    gattt[...] = gatt[...].T

    def heads(group, carry):
        lanes = pl.ds(pl.multiple_of(group * 128, 128), 128)
        lanes_k = pl.ds(pl.multiple_of(FEAT + group * 128, 128), 128)
        lanes_v = pl.ds(pl.multiple_of(2 * FEAT + group * 128, 128), 128)
        q_group, k_group, v_group = proj[:, lanes], proj[:, lanes_k], proj[:, lanes_v]
        ga_group = gatt[:, lanes]
        lane_head = iota((1, 128), 1) // HEAD_SIZE
        for j in range(4):
            head = group * 4 + j
            rows = pl.ds(pl.multiple_of(head * HEAD_SIZE, HEAD_SIZE), HEAD_SIZE)
            rows_k = pl.ds(pl.multiple_of(FEAT + head * HEAD_SIZE, HEAD_SIZE), HEAD_SIZE)
            rows_v = pl.ds(pl.multiple_of(2 * FEAT + head * HEAD_SIZE, HEAD_SIZE), HEAD_SIZE)
            mine = (lane_head == j).astype(F32).astype(BF16)
            scores = mm(k_group * mine, q_group, NT) * SCORE_SCALE
            scores = jnp.where(allow[...] > 0.5, scores + bias[head], MASKED)
            exponent = jnp.exp(scores - jnp.max(scores, axis=0, keepdims=True))
            probs = exponent * (1.0 / jnp.sum(exponent, axis=0, keepdims=True))
            probs_b = probs.astype(BF16)
            attt[rows, :] = mm(projt[rows_v, :], probs_b).astype(BF16)
            gradt[rows_v, :] = mm(gattt[rows, :], probs_b, NT).astype(BF16)
            grad_probs = mm(v_group * mine, ga_group, NT)
            inner = jnp.sum(probs * grad_probs, axis=0, keepdims=True)
            grad_scores = probs * (grad_probs - inner)
            ds[head] = grad_scores
            grad_b = grad_scores.astype(BF16)
            gradt[rows, :] = (mm(projt[rows_k, :], grad_b) * SCORE_SCALE).astype(BF16)
            gradt[rows_k, :] = (mm(projt[rows, :], grad_b, NT) * SCORE_SCALE).astype(BF16)
        return carry

    lax.fori_loop(0, 4, heads, 0)

    def half_block(which, block):
        if block < 3:
            rows = pl.ds(pl.multiple_of(block * FEAT + which * 256, 256), 256)
            out = mm(nrmt[...], gradt[rows, :], NT)
            return out[:, 0:128], out[:, 128:256]
        rows = pl.ds(pl.multiple_of(which * 256, 256), 256)
        out = mm(attt[rows, :], cotf[...])
        return (
            jnp.concatenate([out[:, 0:128], out[:, 128:256]], axis=0),
            jnp.concatenate([out[:, 256:384], out[:, 384:512]], axis=0),
        )

    core_copies = []
    for block in range(4):
        first, second = half_block(1 - core, block)
        sib_send[0, 512 * block:512 * block + 512, :] = first.astype(BF16)
        sib_send[1, 512 * block:512 * block + 512, :] = second.astype(BF16)
        made = copy(
            sib_send.at[:, pl.ds(512 * block, 512)], sib_recv.at[:, pl.ds(512 * block, 512)],
            CORE + block, sibling,
        )
        made.start()
        core_copies.append(made)
    for block in range(4):
        first, second = half_block(core, block)
        own_half[0, 512 * block:512 * block + 512, :] = first
        own_half[1, 512 * block:512 * block + 512, :] = second
    for block in range(4):
        core_copies[block].wait_recv()

        def add_block(step, carry, block=block):
            rows = pl.ds(pl.multiple_of(512 * block + 128 * step, 128), 128)
            pay[:, rows, :] = (own_half[:, rows, :] + sib_recv[:, rows, :].astype(F32)).astype(BF16)
            return carry

        lax.fori_loop(0, 4, add_block, 0)

    def rows_of(start, count):
        return pl.ds(pl.multiple_of(start, 16), count)

    major, minor = (x, y), (y, x)
    at_major, at_minor = (at_x, at_y), (at_y, at_x)
    rs1 = [[], []]
    for d in range(1, 4):
        for p in range(2):
            to = (major[p] + d) % 4
            made = copy(pay.at[p, rows_of(512 * to, 512)], r1.at[p, d - 1], RS1 + 3 * p + d - 1, at_major[p](to))
            made.start()
            rs1[p].append(made)

    ones = iota((96, WT), 0)
    sub = iota((8, WT), 0)

    def scatter(step, total):
        rows = pl.ds(pl.multiple_of(8 * step, 8), 8)
        indices = relt[rows, 0:WT]
        for k in range(8):
            index = indices[k:k + 1, :]
            upper = (ones == (index >> 3)).astype(F32).astype(BF16)
            match = sub == (index & 7)
            pieces = [
                jnp.where(match, jnp.broadcast_to(ds[h, rows, :][k:k + 1, :], (8, WT)), 0.0)
                for h in range(HEADS)
            ]
            total = total + mm(upper, jnp.concatenate(pieces, axis=0).astype(BF16), NT)
        return total

    total = lax.fori_loop(0, WT // 8, scatter, jnp.zeros((96, 128), F32))
    tsum[...] = total.T
    spread = (iota((96, 768), 1) // 8 == iota((96, 768), 0)).astype(F32)
    wide = lax.dot_general(tsum[...], spread, NN, precision=lax.Precision.HIGHEST, preferred_element_type=F32)
    wide = jnp.where(iota((128, 768), 1) % 8 == iota((128, 768), 0) % 8, wide, 0.0)
    wide = jnp.sum(wide.reshape(HEADS, 8, 768), axis=1)
    tb[...] = jnp.zeros((128, 128), F32)
    for c in range(6):
        tb[16 * c:16 * c + 16, :] = wide[:, 128 * c:128 * c + 128]

    grad_normed = mm(gradt[...].T, wqkv_ref[...], NT)
    standard = std[...]
    grad_gain = jnp.sum(grad_normed * standard, axis=0, keepdims=True)
    for c in range(4):
        tb[96 + c:97 + c, :] = grad_gain[:, 128 * c:128 * c + 128]
    tcore = copy(tb.at[rows_of(64 * (1 - core), 64)], rt0, TCORE, sibling)
    tcore.start()
    grad_hat = grad_normed * gain_ref[...]
    grad_in = istd[...] * (
        grad_hat
        - jnp.mean(grad_hat, axis=-1, keepdims=True)
        - standard * jnp.mean(grad_hat * standard, axis=-1, keepdims=True)
    )
    back_send[...] = grad_in.astype(BF16).reshape(6, 12, 2, FEAT)
    back = []
    returns = (
        ((0, 6), (3, 0), (east, lat)),
        ((3, 0), (0, 6), (lon, north)),
        ((3, 6), (0, 0), (east, north)),
    )
    for n, (source, target, device) in enumerate(returns):
        made = copy(
            back_send.at[pl.ds(source[0], 3), pl.ds(source[1], 6)],
            back_recv.at[pl.ds(target[0], 3), pl.ds(target[1], 6)],
            BACK + n, device,
        )
        made.start()
        back.append(made)
    ginf[...] = grad_in.reshape(6, 12, 2, FEAT)

    rs2 = [[], []]
    for p in range(2):
        for made in rs1[p]:
            made.wait_recv()

        def add_one(step, carry, p=p):
            rows = pl.ds(pl.multiple_of(128 * step, 128), 128)
            own = pl.ds(pl.multiple_of(512 * major[p] + 128 * step, 128), 128)
            value = pay[p, own, :].astype(F32)
            for d in range(3):
                value = value + r1[p, d, rows, :].astype(F32)
            s1[p, rows, :] = value.astype(BF16)
            return carry

        lax.fori_loop(0, 4, add_one, 0)
        for d in range(1, 4):
            to = (minor[p] + d) % 4
            made = copy(s1.at[p, rows_of(128 * to, 128)], r2.at[p, d - 1], RS2 + 3 * p + d - 1, at_minor[p](to))
            made.start()
            rs2[p].append(made)

    tcore.wait_recv()
    t1[...] = tb[rows_of(64 * core, 64), :] + rt0[...]
    tx = []
    for d in range(1, 4):
        to = (x + d) % 4
        made = copy(t1.at[rows_of(16 * to, 16)], rt1.at[d - 1], TX + d - 1, at_x(to))
        made.start()
        tx.append(made)

    rs3 = [[], []]
    for p in range(2):
        for made in rs2[p]:
            made.wait_recv()
        value = s1[p, rows_of(128 * minor[p], 128), :].astype(F32)
        for d in range(3):
            value = value + r2[p, d].astype(F32)
        s2[p] = value.astype(BF16)
        for d in range(1, 8):
            to = (z + d) % 8
            made = copy(s2.at[p, rows_of(16 * to, 16)], r3.at[p, d - 1], RS3 + 7 * p + d - 1, at_z(to))
            made.start()
            rs3[p].append(made)

    for made in tx:
        made.wait_recv()
    value = t1[rows_of(16 * x, 16), :]
    for d in range(3):
        value = value + rt1[d]
    t2[...] = value
    ty = []
    for d in range(1, 4):
        made = copy(t2, rt2.at[d - 1], TY + d - 1, at_y((y + d) % 4))
        made.start()
        ty.append(made)

    base1 = [512 * major[p] for p in range(2)]
    base2 = [base1[p] + 128 * minor[p] for p in range(2)]
    base3 = [base2[p] + 16 * z for p in range(2)]

    def gather(p, base, count, index, device):
        part = big_ref.at[core, p, rows_of(base, count)]
        made = copy(part, part, index, device)
        made.start()
        return made

    ag1 = [[], []]
    for p in range(2):
        for made in rs3[p]:
            made.wait_recv()
        value = s2[p, rows_of(16 * z, 16), :].astype(F32)
        for d in range(7):
            value = value + r3[p, d].astype(F32)
        big_ref[core, p, rows_of(base3[p], 16), :] = value.astype(BF16)
        for d in range(1, 8):
            ag1[p].append(gather(p, base3[p], 16, AG1 + 7 * p + d - 1, at_z((z + d) % 8)))

    for made in ty:
        made.wait_recv()
    value = t2[...]
    for d in range(3):
        value = value + rt2[d]
    t3[...] = value
    tz = []
    for d in range(1, 8):
        made = copy(t3, rt3.at[d - 1], TZ + d - 1, at_z((z + d) % 8))
        made.start()
        tz.append(made)

    ag2 = [[], []]
    for p in range(2):
        for made in ag1[p]:
            made.wait_recv()
        for d in range(1, 4):
            ag2[p].append(gather(p, base2[p], 128, AG2 + 3 * p + d - 1, at_minor[p]((minor[p] + d) % 4)))

    for made in tz:
        made.wait_recv()
    value = t3[...]
    for d in range(7):
        value = value + rt3[d]
    trow = 64 * core + 16 * x
    tf[rows_of(trow, 16), :] = value * GRAD_SCALE
    txg = []
    for d in range(1, 4):
        made = copy(tf.at[rows_of(trow, 16)], tf.at[rows_of(trow, 16)], TXG + d - 1, at_x((x + d) % 4))
        made.start()
        txg.append(made)

    ag3 = [[], []]
    sib = []

    def forward(p, block, index):
        part = big_ref.at[core, p, rows_of(512 * block, 512)]
        made = copy(part, part, index, sibling)
        made.start()
        sib.append(made)

    for p in range(2):
        for made in ag2[p]:
            made.wait_recv()
        for d in range(1, 4):
            ag3[p].append(gather(p, base1[p], 512, AG3 + 3 * p + d - 1, at_major[p]((major[p] + d) % 4)))
        forward(p, major[p], SIB + 4 * p)

    for made in back:
        made.wait_recv()
    gin_ref[0:3, 0:6] = back_recv[0:3, 0:6].astype(F32)
    gin_ref[0:3, 6:12] = back_recv[0:3, 6:12].astype(F32)
    gin_ref[3:6, 0:6] = back_recv[3:6, 0:6].astype(F32)
    gin_ref[3:6, 6:12] = ginf[0:3, 0:6]

    for made in txg:
        made.wait_recv()
    thalf = tf.at[rows_of(64 * core, 64)]
    tsib = copy(thalf, thalf, TSIB, sibling)
    tsib.start()

    for d in range(1, 4):
        for p in range(2):
            ag3[p][d - 1].wait_recv()
            forward(p, (major[p] + 4 - d) % 4, SIB + 4 * p + d)

    tsib.wait_recv()
    for c in range(5):
        table_ref[:, 128 * c:128 * c + 128] = tf[16 * c:16 * c + 16, :]
    table_ref[:, 640:NBIAS] = tf[80:96, 0:NBIAS - 640]
    for c in range(4):
        ggain_ref[:, 128 * c:128 * c + 128] = tf[96 + c:97 + c, :]

    for made in sib:
        made.wait_recv()
    every = halo + core_copies + rs1[0] + rs1[1] + rs2[0] + rs2[1] + rs3[0] + rs3[1]
    every += ag1[0] + ag1[1] + ag2[0] + ag2[1] + ag3[0] + ag3[1] + sib
    every += [tcore] + tx + ty + tz + txg + [tsib] + back
    for made in every:
        made.wait_send()


def per_device(inputs, cotangent, pad_mask, rel_index, bias_table, ln_gain, w_qkv, w_out):
    vmem = pl.BlockSpec(memory_space=pltpu.VMEM)
    anywhere = pl.BlockSpec(memory_space=pl.ANY)
    big, grad_in, table, gain = pl.pallas_call(
        body,
        out_shape=(
            jax.ShapeDtypeStruct((2, 2, 2048, 128), BF16),
            jax.ShapeDtypeStruct((6, 12, 2, FEAT), F32),
            jax.ShapeDtypeStruct((HEADS, NBIAS), F32),
            jax.ShapeDtypeStruct((1, FEAT), F32),
        ),
        in_specs=[anywhere, anywhere] + [vmem] * 6,
        out_specs=[vmem] * 4,
        scratch_shapes=[
            pltpu.VMEM((6, 12, 2, FEAT), BF16),
            pltpu.VMEM((6, 12, 2, FEAT), BF16),
            pltpu.VMEM((3, 6, 12), I32),
            pltpu.VMEM((32, 128), F32),
            pltpu.VMEM((WT, 256), I32),
            pltpu.VMEM((HEADS, 1, 768), F32),
            pltpu.VMEM((HEADS, WT, WT), F32),
            pltpu.VMEM((WT, WT), F32),
            pltpu.VMEM((WT, FEAT), F32),
            pltpu.VMEM((WT, 1), F32),
            pltpu.VMEM((WT, FEAT), BF16),
            pltpu.VMEM((FEAT, WT), BF16),
            pltpu.VMEM((WT, FEAT), BF16),
            pltpu.VMEM((WT, 3 * FEAT), BF16),
            pltpu.VMEM((3 * FEAT, WT), BF16),
            pltpu.VMEM((WT, FEAT), BF16),
            pltpu.VMEM((FEAT, WT), BF16),
            pltpu.VMEM((FEAT, WT), BF16),
            pltpu.VMEM((3 * FEAT, WT), BF16),
            pltpu.VMEM((HEADS, WT, WT), F32),
            pltpu.VMEM((2, 2048, 128), BF16),
            pltpu.VMEM((2, 2048, 128), BF16),
            pltpu.VMEM((2, 2048, 128), F32),
            pltpu.VMEM((2, 2048, 128), BF16),
            pltpu.VMEM((2, 3, 512, 128), BF16),
            pltpu.VMEM((2, 512, 128), BF16),
            pltpu.VMEM((2, 3, 128, 128), BF16),
            pltpu.VMEM((2, 128, 128), BF16),
            pltpu.VMEM((2, 7, 16, 128), BF16),
            pltpu.VMEM((128, 96), F32),
            pltpu.VMEM((128, 128), F32),
            pltpu.VMEM((64, 128), F32),
            pltpu.VMEM((64, 128), F32),
            pltpu.VMEM((3, 16, 128), F32),
            pltpu.VMEM((16, 128), F32),
            pltpu.VMEM((3, 16, 128), F32),
            pltpu.VMEM((16, 128), F32),
            pltpu.VMEM((7, 16, 128), F32),
            pltpu.VMEM((128, 128), F32),
            pltpu.VMEM((6, 12, 2, FEAT), BF16),
            pltpu.VMEM((6, 12, 2, FEAT), BF16),
            pltpu.VMEM((6, 12, 2, FEAT), F32),
            pltpu.SemaphoreType.DMA((SEMS,)),
            pltpu.SemaphoreType.DMA((SEMS,)),
        ],
        compiler_params=pltpu.CompilerParams(
            collective_id=0, has_side_effects=True, vmem_limit_bytes=48 * 1024 * 1024
        ),
    )(
        inputs.transpose(1, 2, 0, 3),
        cotangent.transpose(1, 2, 0, 3),
        pad_mask,
        rel_index,
        bias_table.T,
        ln_gain.reshape(1, FEAT),
        w_qkv,
        w_out,
    )
    wqkv = big[:, :, :1536].reshape(2, 2, 3, FEAT, 128).transpose(3, 2, 0, 1, 4).reshape(FEAT, 3 * FEAT)
    wout = big[:, :, 1536:].reshape(2, 2, 2, 256, 128).transpose(0, 3, 1, 2, 4).reshape(FEAT, FEAT)
    return (
        grad_in.transpose(2, 0, 1, 3),
        gain.reshape(FEAT),
        wqkv.astype(F32) * GRAD_SCALE,
        wout.astype(F32) * GRAD_SCALE,
        table.T,
    )


def solution(mesh):
    in_specs = (
        P(None, "lat", "lon", None),
        P(None, "lat", "lon", None),
        P("lat", "lon"),
        P(),
        P(),
        P(),
        P(),
        P(),
    )
    out_specs = (P(None, "lat", "lon", None), P(), P(), P(), P())
    return jax.shard_map(
        per_device, mesh=mesh, in_specs=in_specs, out_specs=out_specs, check_vma=False
    )
```

time: 427 us -> 93.8 us (0.22)
  waiting for transfers between devices: 147 us -> 0 us
  matrix products: 79.7 us -> 0 us
  blocking collectives: 77 us -> 0 us
  Pallas kernels: 0 us -> 71 us
  local copies, waits for them, and re-layouts: 65.2 us -> 21.4 us
  starting transfers between devices: 19.7 us -> 0 us
  other arithmetic: 18.3 us -> 0.32 us
  between operations: 14.3 us -> 0.68 us
    psum x1 -> x0, waiting for transfers between devices: 137 us -> none  [per_device(): lax.psum((grad_parts[0], grad_parts[1], grad_parts[2], grad_parts[3]), ('...]
    dot_general x47 -> x0, matrix products: 79.7 us -> none  [the longest x18 45.5 us: lookup_block(): return jnp.dot(one_hot, bias_table, precision=lax.Precision.HIGHEST)]
    psum x1 -> x0, blocking collectives: 77 us -> none  [per_device(): lax.psum((grad_parts[0], grad_parts[1], grad_parts[2], grad_parts[3]), ('...]
    pallas_call x0 -> x1, Pallas kernels: none -> 71 us  [per_device(): pl.pallas_call(body, out_shape=(jax.ShapeDtypeStruct((2, 2, 2048, 128), B...]
    dynamic_slice x54 -> x0, local copies, waits for them, and re-layouts: 29.7 us -> none  [the longest x36 28.6 us: table_lookup(): looked = lax.map(lookup_block, pair_blocks(rel_index))]
    ppermute x8 -> x0, starting transfers between devices: 19.6 us -> none  [shifted_2(): return lax.ppermute(x, axis, [(i, (i + by) % size) for i in range(size)])]
    mul x6 -> x2, other arithmetic: 11.8 us -> 0.32 us  [the longest x1 0.24 us: per_device(): wqkv.astype(F32) * GRAD_SCALE]
    dynamic_update_slice x36 -> x0, local copies, waits for them, and re-layouts: 10.9 us -> none  [table_lookup(): looked = lax.map(lookup_block, pair_blocks(rel_index))]
  transfers between devices with their start and end apart: 9 -> 0, of which waited for: 4 -> 0; matrix products, arithmetic and copies ran while one was open for 33% -> 0% of each run, Pallas kernels for 0% -> 0%
where the time goes in v1:
time: 93.8 us; the launch traced here: 93.4 us
  Pallas kernels  71 us (76%)
  local copies, waits for them, and re-layouts  21.4 us (23%)
    pallas_call x1, Pallas kernels, per_device(): pl.pallas_call(body, out_shape=(jax.ShapeDtypeStruct((2, 2, 2048, 128), B...  71 us
    mul x2, local copies, waits for them, and re-layouts, per_device(): wqkv.astype(F32) * GRAD_SCALE  9.52 us
    unnamed x19, local copies, waits for them, and re-layouts  9.25 us
    mul x2, local copies, waits for them, and re-layouts, per_device(): wout.astype(F32) * GRAD_SCALE  2.62 us

profile of v1, /device:TPU:1, one launch (start us, length us, event | category | flops | bytes accessed | tf_op | source)
XLA Modules:
  0.0 93.4 jit_solution(12221171171023494226)
XLA Ops:
  0.6 0.0 copy-start
  0.6 1.4 %copy-done = bf16[512,1536]{1,0:T(8,128)(2,1)S(1)} copy-done((bf16[512,1536]{1,0:T(8,128)(2,1)S(1)}, bf16[512,1536]{1,0:T(8,128)(2,1)}, u32[]{:S(2)}) %copy-start) | copy-done | bytes 1572888
  2.0 0.0 copy-start.1
  2.0 1.0 %copy-done.1 = bf16[512,512]{1,0:T(8,128)(2,1)S(1)} copy-done((bf16[512,512]{1,0:T(8,128)(2,1)S(1)}, bf16[512,512]{1,0:T(8,128)(2,1)}, u32[]{:S(2)}) %copy-start.1) | copy-done | bytes 524312
  3.1 0.0 copy-start.2
  3.1 0.9 copy-done.2
  4.0 0.0 copy-start.3
  4.0 0.9 copy-done.3
  4.9 0.0 copy-start.4
  4.9 0.9 copy-done.4
  5.8 0.0 copy-start.5
  5.8 0.8 copy-done.5
  6.6 0.0 copy-start.6
  6.6 0.7 copy-done.6
  7.3 0.0 copy-start.7
  7.3 0.7 copy-done.7
  8.0 71.0 %shard_map.119 = (bf16[2,2,2048,128]{3,2,1,0:T(8,128)(2,1)S(1)}, f32[6,12,2,512]{3,2,1,0:T(2,128)S(1)}, f32[16,759]{1,0:T(8,128)S(1)}, f32[1,512]{1,0:T(1,128)S(1)}) custom-call(bf16[6,12,2,512]{3,2,1,0:T(2,128)(2,1)S(1)} %bitcast.14, bf16[6,12,2,512]{3,2,1,0:T(2,128)(2,1)S(1)} %bitcast.15, s32[6,12]{1,0:T(8,128)S(1)} %copy-done.6, ...), custom_call_target="tpu_custom_call" | custom-call | tf_op jit(solution)/shard_map/pallas_call | solution.py:483
  79.0 0.1 convert_multiply_fusion.1
  79.1 0.8 copy.14
  79.9 1.8 %mul.39 = f32[512,512]{1,0:T(8,128)} reshape(f32[2,256,2,2,128]{4,3,2,1,0:T(2,128)S(1)} %copy.14) | data formatting | bytes 2097152 | tf_op jit(solution)/shard_map/mul | solution.py:558
  81.7 0.2 convert_multiply_fusion
  82.0 4.1 %copy.13 = f32[512,3,2,2,128]{4,3,2,1,0:T(2,128)} copy(f32[512,3,2,2,128]{4,0,1,3,2:T(8,128)S(1)} %bitcast.20) | data formatting | bytes 6291456 | tf_op jit(solution)/shard_map/mul | solution.py:557
  86.1 5.5 %mul.34 = f32[512,1536]{1,0:T(8,128)} reshape(f32[512,3,2,2,128]{4,3,2,1,0:T(2,128)} %copy.13) | data formatting | bytes 6291456 | tf_op jit(solution)/shard_map/mul | solution.py:557
  91.5 0.7 copy.18
  92.2 0.6 copy.19
  92.8 0.6 copy.20
Async XLA Ops:
  0.6 1.4 %copy-start = (bf16[512,1536]{1,0:T(8,128)(2,1)S(1)}, bf16[512,1536]{1,0:T(8,128)(2,1)}, u32[]{:S(2)}) copy-start(bf16[512,1536]{1,0:T(8,128)(2,1)} %wqkv_ref.1) | copy-start | bytes 4718596
  2.0 1.0 %copy-start.1 = (bf16[512,512]{1,0:T(8,128)(2,1)S(1)}, bf16[512,512]{1,0:T(8,128)(2,1)}, u32[]{:S(2)}) copy-start(bf16[512,512]{1,0:T(8,128)(2,1)} %wout_ref.1) | copy-start | bytes 1572868
  3.1 0.9 copy-start.2
  4.0 0.9 copy-start.3
  4.9 0.9 copy-start.4
  5.8 0.8 copy-start.5
  6.6 0.7 copy-start.6
  7.3 0.7 copy-start.7

commit v2 on v1

--- a/solution.py
+++ b/solution.py
@@ -51,13 +51,14 @@
 
 
 def body(
-    x_ref, cot_ref, pad_ref, rel_ref, bias_ref, gain_ref, wqkv_ref, wout_ref,
+    x_ref, cot_ref, pad_hbm, rel_hbm, bias_hbm, gain_hbm, wqkv_hbm, wout_hbm,
     big_ref, gin_ref, table_ref, ggain_ref,
-    xw, cw, pads, padf, relt, tab, bias, allow, std, istd, nrm, nrmt, cotf,
+    pad_ref, rel_ref, bias_ref, gain_ref, wqkv_ref, wout_ref,
+    xw, cw, pads, padf, relt, tab, edge, edge_bias, bias, allow, std, istd, nrm, nrmt, cotf,
     proj, projt, gatt, gattt, attt, gradt, ds,
     sib_send, sib_recv, own_half, pay, r1, s1, r2, s2, r3,
     tsum, tb, rt0, t1, rt1, t2, rt2, t3, rt3, tf,
-    back_send, back_recv, ginf, ssem, rsem,
+    back_send, back_recv, ginf, ssem, rsem, lsem,
 ):
     lon = lax.axis_index("lon")
     lat = lax.axis_index("lat")
@@ -79,12 +80,29 @@
     west, east = (lon + 15) % 16, (lon + 1) % 16
     south, north = (lat + 15) % 16, (lat + 1) % 16
 
+    started = []
+
     def copy(src, dst, index, device):
         made = pltpu.make_async_remote_copy(
             src_ref=src, dst_ref=dst, send_sem=ssem.at[index], recv_sem=rsem.at[index],
             device_id=device, device_id_type=MESH,
         )
+        started.append(made)
         return made
+
+    loads = {}
+    for n, (name, src, dst) in enumerate((
+        ("rel", rel_hbm, rel_ref),
+        ("bias", bias_hbm, bias_ref),
+        ("pad", pad_hbm, pad_ref),
+        ("x", x_ref.at[pl.ds(3, 3), pl.ds(6, 6)], xw.at[pl.ds(0, 3), pl.ds(0, 6)]),
+        ("cot", cot_ref.at[pl.ds(3, 3), pl.ds(6, 6)], cw.at[pl.ds(0, 3), pl.ds(0, 6)]),
+        ("gain", gain_hbm, gain_ref),
+        ("wqkv", wqkv_hbm, wqkv_ref),
+        ("wout", wout_hbm, wout_ref),
+    )):
+        loads[name] = pltpu.make_async_copy(src, dst, lsem.at[n])
+        loads[name].start()
 
     barrier = pltpu.get_barrier_semaphore()
     partners = [sibling, (west, lat), (lon, south), (west, south), (east, lat), (lon, north), (east, north)]
@@ -108,11 +126,11 @@
                 window.at[pl.ds(target[0], 3), pl.ds(target[1], 6)],
                 HALO + 3 * n + m, device,
             ))
-        halo.append(copy(pad_ref, pads.at[n], HALO + 3 * n + 2, device))
+        halo.append(copy(pad_hbm, pads.at[n], HALO + 3 * n + 2, device))
     for made in halo:
         made.start()
-    pltpu.sync_copy(x_ref.at[pl.ds(3, 3), pl.ds(6, 6)], xw.at[pl.ds(0, 3), pl.ds(0, 6)])
-    pltpu.sync_copy(cot_ref.at[pl.ds(3, 3), pl.ds(6, 6)], cw.at[pl.ds(0, 3), pl.ds(0, 6)])
+    for name in ("rel", "bias"):
+        loads[name].wait()
 
     token = iota((WT, WT), 0)
     order = (iota((WT, WT), 1) == (token % 2) * 72 + token // 2).astype(BF16)
@@ -125,25 +143,51 @@
     for head in range(HEADS):
         tab[head, :, :NBIAS] = bias_ref[head:head + 1, :]
 
-    def lookup(head, carry):
-        for part in range(2):
-            index = relt[:, 128 * part:128 * part + 128]
-            lane, chunk = index & 127, index >> 7
-            found = jnp.zeros((WT, 128), F32)
+    def gather_heads(index, put):
+        lane, chunk = index & 127, index >> 7
+        inside = [chunk == c for c in range(6)]
+        for head in range(HEADS):
+            found = jnp.zeros(index.shape, F32)
             for c in range(6):
-                row = jnp.broadcast_to(tab[head, :, 128 * c:128 * c + 128], (WT, 128))
+                row = jnp.broadcast_to(tab[head, :, 128 * c:128 * c + 128], index.shape)
                 taken = jnp.take_along_axis(row, lane, axis=1, mode="promise_in_bounds")
-                found = jnp.where(chunk == c, taken, found)
-            if part == 0:
-                bias[head, :, 0:128] = found
-            else:
-                bias[head, :, 128:WT] = found[:, 0:WT - 128]
+                found = jnp.where(inside[c], taken, found)
+            put(head, found)
+
+    def lookup(step, carry):
+        rows = pl.ds(pl.multiple_of(8 * step, 8), 8)
+
+        def put(head, found):
+            bias[head, rows, 0:128] = found
+
+        gather_heads(relt[rows, 0:128], put)
         return carry
 
-    lax.fori_loop(0, HEADS, lookup, 0)
+    lax.fori_loop(0, WT // 8, lookup, 0)
+    rest_index = relt[:, 128:256].T
+    for part in range(2):
+        edge[part] = rest_index[0:16, 0:128] if part == 0 else jnp.concatenate(
+            [rest_index[0:16, 128:WT], jnp.zeros((16, 256 - WT), I32)], axis=1
+        )
+
+    def lookup_rest(step, carry):
+        part, half = step // 2, pl.ds(pl.multiple_of(8 * (step % 2), 8), 8)
+
+        def put(head, found):
+            edge_bias[head, part, half, :] = found
+
+        gather_heads(edge[part, half, :], put)
+        return carry
+
+    lax.fori_loop(0, 4, lookup_rest, 0)
+    for head in range(HEADS):
+        bias[head, 0:128, 128:WT] = edge_bias[head, 0].T
+        bias[head, 128:WT, 128:WT] = edge_bias[head, 1].T[0:16, :]
 
     for made in halo:
         made.wait_recv()
+    for name in ("pad", "x", "cot", "gain", "wqkv", "wout"):
+        loads[name].wait()
 
     padf[...] = jnp.zeros((32, 128), F32)
     padf[0:6, 0:12] = pad_ref[...].astype(F32)
@@ -470,16 +514,44 @@
 
     for made in sib:
         made.wait_recv()
-    every = halo + core_copies + rs1[0] + rs1[1] + rs2[0] + rs2[1] + rs3[0] + rs3[1]
-    every += ag1[0] + ag1[1] + ag2[0] + ag2[1] + ag3[0] + ag3[1] + sib
-    every += [tcore] + tx + ty + tz + txg + [tsib] + back
-    for made in every:
+    for made in started:
         made.wait_send()
+
+
+def widen(big, gin, table, gain, gin_out, gain_out, wqkv_out, wout_out, table_out, wqkv, wout, sem):
+    made = [
+        pltpu.make_async_copy(gin, gin_out, sem.at[0]),
+        pltpu.make_async_copy(gain, gain_out, sem.at[1]),
+        pltpu.make_async_copy(table, table_out, sem.at[2]),
+    ]
+    for one in made:
+        one.start()
+    for step in range(4):
+        rows = slice(128 * step, 128 * step + 128)
+        for block in range(3):
+            for core in range(2):
+                for p in range(2):
+                    lanes = slice(512 * block + 256 * core + 128 * p, 512 * block + 256 * core + 128 * p + 128)
+                    source = slice(512 * block + 128 * step, 512 * block + 128 * step + 128)
+                    wqkv[rows, lanes] = big[core, p, source, :].astype(F32) * GRAD_SCALE
+        one = pltpu.make_async_copy(wqkv.at[pl.ds(128 * step, 128)], wqkv_out.at[pl.ds(128 * step, 128)], sem.at[3 + step])
+        one.start()
+        made.append(one)
+        core, half = step // 2, step % 2
+        for p in range(2):
+            for u in range(2):
+                source = slice(1536 + 256 * u + 128 * half, 1536 + 256 * u + 128 * half + 128)
+                wout[rows, 256 * p + 128 * u:256 * p + 128 * u + 128] = big[core, p, source, :].astype(F32) * GRAD_SCALE
+        one = pltpu.make_async_copy(wout.at[pl.ds(128 * step, 128)], wout_out.at[pl.ds(128 * step, 128)], sem.at[7 + step])
+        one.start()
+        made.append(one)
+    for one in made:
+        one.wait()
 
 
 def per_device(inputs, cotangent, pad_mask, rel_index, bias_table, ln_gain, w_qkv, w_out):
     vmem = pl.BlockSpec(memory_space=pltpu.VMEM)
-    anywhere = pl.BlockSpec(memory_space=pl.ANY)
+    hbm = pl.BlockSpec(memory_space=pltpu.HBM)
     big, grad_in, table, gain = pl.pallas_call(
         body,
         out_shape=(
@@ -488,15 +560,23 @@
             jax.ShapeDtypeStruct((HEADS, NBIAS), F32),
             jax.ShapeDtypeStruct((1, FEAT), F32),
         ),
-        in_specs=[anywhere, anywhere] + [vmem] * 6,
+        in_specs=[hbm] * 8,
         out_specs=[vmem] * 4,
         scratch_shapes=[
+            pltpu.VMEM((6, 12), I32),
+            pltpu.VMEM((WT, WT), I32),
+            pltpu.VMEM((HEADS, NBIAS), F32),
+            pltpu.VMEM((1, FEAT), F32),
+            pltpu.VMEM((FEAT, 3 * FEAT), BF16),
+            pltpu.VMEM((FEAT, FEAT), BF16),
             pltpu.VMEM((6, 12, 2, FEAT), BF16),
             pltpu.VMEM((6, 12, 2, FEAT), BF16),
             pltpu.VMEM((3, 6, 12), I32),
             pltpu.VMEM((32, 128), F32),
             pltpu.VMEM((WT, 256), I32),
             pltpu.VMEM((HEADS, 1, 768), F32),
+            pltpu.VMEM((2, 16, 128), I32),
+            pltpu.VMEM((HEADS, 2, 16, 128), F32),
             pltpu.VMEM((HEADS, WT, WT), F32),
             pltpu.VMEM((WT, WT), F32),
             pltpu.VMEM((WT, FEAT), F32),
@@ -535,29 +615,45 @@
             pltpu.VMEM((6, 12, 2, FEAT), F32),
             pltpu.SemaphoreType.DMA((SEMS,)),
             pltpu.SemaphoreType.DMA((SEMS,)),
+            pltpu.SemaphoreType.DMA((8,)),
         ],
         compiler_params=pltpu.CompilerParams(
             collective_id=0, has_side_effects=True, vmem_limit_bytes=48 * 1024 * 1024
         ),
     )(
-        inputs.transpose(1, 2, 0, 3),
-        cotangent.transpose(1, 2, 0, 3),
-        pad_mask,
-        rel_index,
-        bias_table.T,
-        ln_gain.reshape(1, FEAT),
-        w_qkv,
-        w_out,
+        *(
+            pltpu.with_memory_space_constraint(one, pltpu.HBM)
+            for one in (
+                inputs.transpose(1, 2, 0, 3),
+                cotangent.transpose(1, 2, 0, 3),
+                pad_mask,
+                rel_index,
+                bias_table.T,
+                ln_gain.reshape(1, FEAT),
+                w_qkv,
+                w_out,
+            )
+        )
     )
-    wqkv = big[:, :, :1536].reshape(2, 2, 3, FEAT, 128).transpose(3, 2, 0, 1, 4).reshape(FEAT, 3 * FEAT)
-    wout = big[:, :, 1536:].reshape(2, 2, 2, 256, 128).transpose(0, 3, 1, 2, 4).reshape(FEAT, FEAT)
-    return (
-        grad_in.transpose(2, 0, 1, 3),
-        gain.reshape(FEAT),
-        wqkv.astype(F32) * GRAD_SCALE,
-        wout.astype(F32) * GRAD_SCALE,
-        table.T,
-    )
+    grad_in, gain, wqkv, wout, table = pl.pallas_call(
+        widen,
+        out_shape=(
+            jax.ShapeDtypeStruct((6, 12, 2, FEAT), F32),
+            jax.ShapeDtypeStruct((1, FEAT), F32),
+            jax.ShapeDtypeStruct((FEAT, 3 * FEAT), F32),
+            jax.ShapeDtypeStruct((FEAT, FEAT), F32),
+            jax.ShapeDtypeStruct((HEADS, NBIAS), F32),
+        ),
+        in_specs=[vmem] * 4,
+        out_specs=[hbm] * 5,
+        scratch_shapes=[
+            pltpu.VMEM((FEAT, 3 * FEAT), F32),
+            pltpu.VMEM((FEAT, FEAT), F32),
+            pltpu.SemaphoreType.DMA((11,)),
+        ],
+        compiler_params=pltpu.CompilerParams(vmem_limit_bytes=24 * 1024 * 1024),
+    )(big, grad_in, table, gain)
+    return grad_in.transpose(2, 0, 1, 3), gain.reshape(FEAT), wqkv, wout, table.T
 
 
 def solution(mesh):

time: 93.8 us -> 68.7 us (0.73)
  local copies, waits for them, and re-layouts: 21.4 us -> 0 us
  Pallas kernels: 71 us -> 68 us
    mul x4 -> x0, local copies, waits for them, and re-layouts: 12.1 us -> none  [the longest x2 9.52 us: per_device(): wqkv.astype(F32) * GRAD_SCALE]
    unnamed x19 -> x0, local copies, waits for them, and re-layouts: 9.25 us -> none
    pallas_call x1, Pallas kernels: 71 us -> 65.8 us  [per_device(): pl.pallas_call(body, out_shape=(jax.ShapeDtypeStruct((2, 2, 2048, 128), B...]
    pallas_call x0 -> x1, Pallas kernels: none -> 2.21 us  [per_device(): pl.pallas_call(widen, out_shape=(jax.ShapeDtypeStruct((6, 12, 2, FEAT), F...]
where the time goes in v2:
time: 68.7 us
  Pallas kernels  68 us (99%)
    pallas_call x1, Pallas kernels, per_device(): pl.pallas_call(body, out_shape=(jax.ShapeDtypeStruct((2, 2, 2048, 128), B...  65.8 us
    pallas_call x1, Pallas kernels, per_device(): pl.pallas_call(widen, out_shape=(jax.ShapeDtypeStruct((6, 12, 2, FEAT), F...  2.21 us

profile of v2, /device:TPU:1, one launch (start us, length us, event | category | flops | bytes accessed | tf_op | source)
XLA Modules:
  0.0 68.7 jit_solution(9770871973648323762)
XLA Ops:
  0.6 65.8 %shard_map.119 = (bf16[2,2,2048,128]{3,2,1,0:T(8,128)(2,1)S(1)}, f32[6,12,2,512]{3,2,1,0:T(2,128)S(1)}, f32[16,759]{1,0:T(8,128)S(1)}, f32[1,512]{1,0:T(1,128)S(1)}) custom-call(bf16[6,12,2,512]{3,2,1,0:T(2,128)(2,1)} %bitcast.7, bf16[6,12,2,512]{3,2,1,0:T(2,128)(2,1)} %bitcast.8, s32[6,12]{1,0:T(8,128)} %pad_hbm.1, s32[144,144]{1,0:T(8,128)} %rel_hbm.1, ...), custom_call_target="tpu_custom_call" | custom-call | tf_op jit(solution)/shard_map/pallas_call | solution.py:555
  66.4 2.2 %shard_map.120 = (f32[6,12,2,512]{3,2,1,0:T(2,128)}, f32[1,512]{1,0:T(1,128)}, f32[512,1536]{1,0:T(8,128)}, f32[512,512]{1,0:T(8,128)}, f32[16,759]{1,0:T(8,128)}) custom-call(bf16[2,2,2048,128]{3,2,1,0:T(8,128)(2,1)S(1)} %get-tuple-element.14.big, f32[6,12,2,512]{3,2,1,0:T(2,128)S(1)} %get-tuple-element.15.gin, f32[16,759]{1,0:T(8,128)S(1)} %get-tuple-element.16.table, ...), custom_call_target="tpu_custom_call" | custom-call | tf_op jit(solution)/shard_map/pallas_call | solution.py:638

commit v3 on v2

v3 whole, which is shorter than its diff:
```python
import jax
import jax.numpy as jnp
from jax import lax
from jax.experimental import pallas as pl
from jax.experimental.pallas import tpu as pltpu
from jax.sharding import PartitionSpec as P

F32 = jnp.float32
BF16 = jnp.bfloat16
I32 = jnp.int32
MESH = pl.DeviceIdType.MESH

EPSILON = 1e-05
MASKED = -30000.0
WT = 144
FEAT = 512
HEADS = 16
HEAD_SIZE = 32
NBIAS = 759
SCORE_SCALE = HEAD_SIZE ** (-0.5)
GRAD_SCALE = 36864.0 ** (-0.5)

NN = (((1,), (0,)), ((), ()))
NT = (((1,), (1,)), ((), ()))

XS, COTS, PADS, PAIR, RS1, RS2, RS3, AG1, AG2, AG3, SIB = 0, 1, 2, 5, 9, 12, 13, 14, 15, 16, 17
TX, TY, TZ, TXG, TSIB, BACK = 18, 19, 20, 21, 22, 23
SENDS = 24
R_RS1, R_RS2, R_RS3, R_AG1, R_AG2, R_AG3, R_SIB = 9, 12, 14, 15, 16, 19, 25
R_TX, R_TY, R_TZ, R_TXG, R_TSIB, R_BACK = 26, 27, 28, 29, 30, 31
RECVS = 32

RING4 = (2, 1, 3)
RING8 = (4, 3, 5, 2, 6, 1, 7)


def mm(a, b, dims=NN):
    return lax.dot_general(a, b, dims, preferred_element_type=F32)


def iota(shape, dim):
    return lax.broadcasted_iota(I32, shape, dim)


def body(
    x_ref, cot_ref, pad_hbm, rel_hbm, bias_hbm, gain_hbm, wqkv_hbm, wout_hbm,
    big_ref, gin_ref, table_ref, ggain_ref,
    pad_ref, rel_ref, bias_ref, gain_ref, wq, wo, wqt, wot,
    xw, cw, pads, padf, relt, tab, edge, edge_bias, bias, validb, allow, std, istd, nrm, nrmt, cotf,
    proj, projt, gatt, gattt, attt, gradt, gnat, probs, ds, gn_send, gn_recv,
    pay, r1, s1, r2, s2, r3, g1,
    tb, rt1, t2, rt2, t3, rt3, tf, tf_recv,
    back_send, back_recv, ginf, ssem, rsem, lsem,
):
    lon = lax.axis_index("lon")
    lat = lax.axis_index("lat")
    z, xhi = lon // 2, lon % 2
    xlo, rest = lat // 8, lat % 8
    y, core = rest // 2, rest % 2
    x = xhi * 2 + xlo

    def at_x(value):
        return (z * 2 + value // 2, (value % 2) * 8 + rest)

    def at_y(value):
        return (lon, xlo * 8 + value * 2 + core)

    def at_z(value):
        return (value * 2 + xhi, lat)

    sibling = (lon, xlo * 8 + y * 2 + (1 - core))
    west, east = (lon + 15) % 16, (lon + 1) % 16
    south, north = (lat + 15) % 16, (lat + 1) % 16

    def send(src, dst, out, into, device):
        pltpu.make_async_remote_copy(
            src_ref=src, dst_ref=dst, send_sem=ssem.at[out], recv_sem=rsem.at[into],
            device_id=device, device_id_type=MESH,
        ).start()

    def arrived(bytes_of, into):
        pltpu.make_async_copy(bytes_of, bytes_of, rsem.at[into]).wait()

    def left(bytes_of, out):
        pltpu.make_async_copy(bytes_of, bytes_of, ssem.at[out]).wait()

    def span(start, count):
        return pl.ds(pl.multiple_of(start, 16), count)

    loads = {}
    heads_at = 256 * core
    parts = [
        ("rel", rel_hbm, rel_ref),
        ("bias", bias_hbm.at[pl.ds(pl.multiple_of(8 * core, 8), 8)], bias_ref),
        ("x", x_ref.at[pl.ds(3, 3), pl.ds(6, 6)], xw.at[pl.ds(0, 3), pl.ds(0, 6)]),
        ("cot", cot_ref.at[pl.ds(3, 3), pl.ds(6, 6)], cw.at[pl.ds(0, 3), pl.ds(0, 6)]),
        ("pad", pad_hbm, pad_ref),
        ("gain", gain_hbm, gain_ref),
        ("wo", wout_hbm.at[span(heads_at, 256)], wo),
    ]
    for block in range(3):
        lanes = pl.ds(pl.multiple_of(FEAT * block + heads_at, 128), 256)
        parts.append(("wq%d" % block, wqkv_hbm.at[:, lanes], wq.at[:, pl.ds(256 * block, 256)]))
    for n, (name, src, dst) in enumerate(parts):
        loads[name] = pltpu.make_async_copy(src, dst, lsem.at[n])
        loads[name].start()

    barrier = pltpu.get_barrier_semaphore()
    partners = [sibling, (west, lat), (lon, south), (west, south), (east, lat), (lon, north), (east, north)]
    partners += [at_x((x + d) % 4) for d in RING4]
    partners += [at_y((y + d) % 4) for d in RING4]
    partners += [at_z((z + d) % 8) for d in RING8]
    for device in partners:
        pl.semaphore_signal(barrier, inc=1, device_id=device, device_id_type=MESH)
    pl.semaphore_wait(barrier, len(partners))

    places = (
        ((0, 0), (3, 6), (west, south)),
        ((3, 0), (0, 6), (west, lat)),
        ((0, 6), (3, 0), (lon, south)),
    )
    three = pl.ds(0, 9)

    def send_quarters(field, window, index):
        for source, target, device in places:
            send(
                field.at[pl.ds(source[0], 3), pl.ds(source[1], 6)],
                window.at[pl.ds(target[0], 3), pl.ds(target[1], 6)],
                index, index, device,
            )

    send_quarters(x_ref, xw, XS)
    for n, (unused, unused, device) in enumerate(places):
        send(pad_hbm, pads.at[n], PADS + n, PADS + n, device)
    send_quarters(cot_ref, cw, COTS)

    for name in ("rel", "bias"):
        loads[name].wait()
    token = iota((WT, WT), 0)
    order = (iota((WT, WT), 1) == (token % 2) * 72 + token // 2).astype(BF16)
    rel = rel_ref[...]
    low = mm(mm(order, (rel & 255).astype(F32).astype(BF16), NT).astype(BF16), order, NT)
    high = mm(mm(order, (rel >> 8).astype(F32).astype(BF16), NT).astype(BF16), order, NT)
    relt[...] = jnp.zeros((WT, 256), I32)
    relt[:, :WT] = (high * 256.0 + low).astype(I32)
    tab[...] = jnp.zeros((8, 1, 768), F32)
    for head in range(8):
        tab[head, :, :NBIAS] = bias_ref[head:head + 1, :]

    def gather_heads(index, put):
        lane, chunk = index & 127, index >> 7
        inside = [chunk == c for c in range(6)]
        for head in range(8):
            found = jnp.zeros(index.shape, F32)
            for c in range(6):
                row = jnp.broadcast_to(tab[head, :, 128 * c:128 * c + 128], index.shape)
                taken = jnp.take_along_axis(row, lane, axis=1, mode="promise_in_bounds")
                found = jnp.where(inside[c], taken, found)
            put(head, found)

    def lookup(step, carry):
        rows = pl.ds(pl.multiple_of(8 * step, 8), 8)

        def put(head, found):
            bias[head, rows, 0:128] = found

        gather_heads(relt[rows, 0:128], put)
        return carry

    lax.fori_loop(0, WT // 8, lookup, 0)
    rest_index = relt[:, 128:256].T
    edge[0] = rest_index[0:16, 0:128]
    edge[1] = jnp.concatenate([rest_index[0:16, 128:WT], jnp.zeros((16, 256 - WT), I32)], axis=1)

    def lookup_rest(step, carry):
        part, half = step // 2, pl.ds(pl.multiple_of(8 * (step % 2), 8), 8)

        def put(head, found):
            edge_bias[head, part, half, :] = found

        gather_heads(edge[part, half, :], put)
        return carry

    lax.fori_loop(0, 4, lookup_rest, 0)
    for head in range(8):
        bias[head, 0:128, 128:WT] = edge_bias[head, 0].T
        bias[head, 128:WT, 128:WT] = edge_bias[head, 1].T[0:16, :]

    for name in ("wo", "wq0", "wq1", "wq2", "pad", "x", "cot", "gain"):
        loads[name].wait()
    wot[...] = wo[...].T
    for block in range(3):
        wqt[256 * block:256 * block + 256, :] = wq[:, 256 * block:256 * block + 256].T

    arrived(xw.at[:, three], XS)
    tokens = xw[...].astype(F32).reshape(WT, FEAT)
    center = tokens - jnp.mean(tokens, axis=-1, keepdims=True)
    variance = jnp.mean(center * center, axis=-1, keepdims=True)
    inv_std = lax.rsqrt(variance + EPSILON)
    standard = center * inv_std
    std[...] = standard
    istd[...] = inv_std
    nrm[0] = (standard * gain_ref[...]).astype(BF16)
    send(nrm.at[0], nrm.at[1], PAIR, PAIR, sibling)

    def project(w):
        proj[w] = mm(nrm[w], wq[...]).astype(BF16)
        projt[w] = proj[w].T
        nrmt[w] = nrm[w].T

    project(0)

    for n in range(3):
        arrived(pads.at[n], PADS + n)
    padf[...] = jnp.zeros((32, 128), F32)
    padf[0:6, 0:12] = pad_ref[...].astype(F32)
    for n, slot_at in enumerate((3, 1, 2)):
        padf[8 * slot_at:8 * slot_at + 6, 0:12] = pads[n].astype(F32)

    def spot(token_at):
        row, col = token_at // 24, (token_at % 24) // 2
        slot = (row >= 3).astype(I32) * 2 + (col >= 6).astype(I32)
        return slot, row + jnp.where(row < 3, 3, -3), col + jnp.where(col < 6, 6, -6)

    slot, source_row, unused = spot(iota((WT, 32), 0))
    row_pick = (iota((WT, 32), 1) == slot * 8 + source_row).astype(BF16)
    unused, unused, source_col = spot(iota((WT, 128), 0))
    picked = mm(row_pick, padf[...].astype(BF16))
    valid = jnp.sum(jnp.where(iota((WT, 128), 1) == source_col, picked, 0.0), axis=1, keepdims=True)
    validb[0] = jnp.broadcast_to(valid, (WT, 128)).astype(BF16)
    send(validb.at[0], validb.at[1], PAIR + 1, PAIR + 1, sibling)

    def see(w):
        key, query = iota((WT, WT), 0), iota((WT, WT), 1)
        across = lat + w * (1 - 2 * core) == 15
        same_group = ((key >= 72) == (query >= 72)) | jnp.logical_not(across)
        valid_key = validb[w].astype(F32)[:, 0:1] > 0.5
        allow[w] = (same_group & (valid_key | (key == query))).astype(F32)

    see(0)
    arrived(cw.at[:, three], COTS)
    cotf[0] = cw[...].reshape(WT, FEAT)
    send(cotf.at[0], cotf.at[1], PAIR + 2, PAIR + 2, sibling)

    def project_cot(w):
        gatt[w] = mm(cotf[w], wot[...]).astype(BF16)
        gattt[w] = gatt[w].T

    project_cot(0)

    def picks(group):
        lanes = [pl.ds(pl.multiple_of(256 * b + group * 128, 128), 128) for b in range(3)]
        head_of_lane = iota((1, 128), 1) // HEAD_SIZE
        mine = [(head_of_lane == j).astype(F32).astype(BF16) for j in range(4)]
        return lanes, mine

    def rows_of(head):
        return [pl.ds(pl.multiple_of(256 * b + head * HEAD_SIZE, HEAD_SIZE), HEAD_SIZE) for b in range(3)]

    def forward_heads(w):
        def step(group, carry):
            lanes, mine = picks(group)
            k_group, ga_group = proj[w, :, lanes[1]], gatt[w, :, lanes[0]]
            qt_group = projt[w, span(128 * group, 128), :]
            grad_values = jnp.zeros((WT, 128), F32)
            for j in range(4):
                head = group * 4 + j
                rows = rows_of(head)
                scores = mm(k_group * mine[j], qt_group) * SCORE_SCALE
                scores = jnp.where(allow[w] > 0.5, scores + bias[head], MASKED)
                exponent = jnp.exp(scores - jnp.max(scores, axis=0, keepdims=True))
                prob = exponent * (1.0 / jnp.sum(exponent, axis=0, keepdims=True))
                probs[w, head] = prob
                prob_b = prob.astype(BF16)
                attt[w, rows[0], :] = mm(projt[w, rows[2], :], prob_b).astype(BF16)
                grad_values = grad_values + mm(prob_b, ga_group * mine[j])
            gnat[w, :, lanes[2]] = grad_values.astype(BF16)
            return carry

        lax.fori_loop(0, 2, step, 0)

    def backward_heads(w):
        def step(group, carry):
            lanes, mine = picks(group)
            q_group, v_group = proj[w, :, lanes[0]], proj[w, :, lanes[2]]
            gat_group = gattt[w, span(128 * group, 128), :]
            grad_keys = jnp.zeros((WT, 128), F32)
            for j in range(4):
                head = group * 4 + j
                rows = rows_of(head)
                prob = probs[w, head]
                grad_probs = mm(v_group * mine[j], gat_group)
                inner = jnp.sum(prob * grad_probs, axis=0, keepdims=True)
                grad_scores = prob * (grad_probs - inner)
                if w == 0:
                    ds[head] = grad_scores
                else:
                    ds[head] = ds[head] + grad_scores
                grad_b = grad_scores.astype(BF16)
                gradt[w, rows[0], :] = (mm(projt[w, rows[1], :], grad_b) * SCORE_SCALE).astype(BF16)
                grad_keys = grad_keys + mm(grad_b, q_group * mine[j])
            gnat[w, :, lanes[1]] = (grad_keys * SCORE_SCALE).astype(BF16)
            return carry

        lax.fori_loop(0, 2, step, 0)

    forward_heads(0)
    arrived(nrm.at[1], PAIR)
    project(1)
    arrived(validb.at[1], PAIR + 1)
    see(1)
    arrived(cotf.at[1], PAIR + 2)
    project_cot(1)
    forward_heads(1)

    major, minor = (x, y), (y, x)
    at_major, at_minor = (at_x, at_y), (at_y, at_x)
    chunk_at = (0, 1024, 1536)
    chunk_rows = (256, 128, 128)

    def columns(block):
        lanes = slice(256 * block, 256 * block + 256)
        return mm(nrmt[0], gnat[0, :, lanes]) + mm(nrmt[1], gnat[1, :, lanes])

    def scatter_pay(e):
        count = chunk_rows[e]
        for d in RING4:
            for p in range(2):
                to = (major[p] + d) % 4
                send(
                    pay.at[p, span(chunk_at[e] + count * to, count)],
                    r1.at[p, d - 1, pl.ds(128 * e + 128 * (e > 0), count)],
                    RS1 + e, R_RS1 + e, at_major[p](to),
                )

    out = columns(2)
    for p in range(2):
        pay[p, 0:512, :] = out[:, 128 * p:128 * p + 128].astype(BF16)
    out = mm(attt[0], cotf[0]) + mm(attt[1], cotf[1])
    for p in range(2):
        for u in range(2):
            lanes = slice(256 * p + 128 * u, 256 * p + 128 * u + 128)
            pay[p, 512 + 256 * u:768 + 256 * u, :] = out[:, lanes].astype(BF16)
    scatter_pay(0)
    backward_heads(0)
    backward_heads(1)
    out = columns(1)
    for p in range(2):
        pay[p, 1024:1536, :] = out[:, 128 * p:128 * p + 128].astype(BF16)
    scatter_pay(1)
    for w in range(2):
        gnat[w, :, 0:256] = gradt[w].T
    out = columns(0)
    for p in range(2):
        pay[p, 1536:2048, :] = out[:, 128 * p:128 * p + 128].astype(BF16)
    scatter_pay(2)

    gn_send[...] = mm(gnat[1], wqt[...])
    send(gn_send, gn_recv, PAIR + 3, PAIR + 3, sibling)
    grad_normed = mm(gnat[0], wqt[...])

    ones = iota((48, WT), 0)
    sub = iota((16, WT), 0)

    def scatter(step, total):
        rows = pl.ds(pl.multiple_of(8 * step, 8), 8)
        indices = relt[rows, 0:WT]
        for k in range(8):
            index = indices[k:k + 1, :]
            upper = (ones == (index >> 4)).astype(F32).astype(BF16)
            match = sub == (index & 15)
            pieces = [
                jnp.where(match, jnp.broadcast_to(ds[h, rows, :][k:k + 1, :], (16, WT)), 0.0)
                for h in range(8)
            ]
            total = total + mm(upper, jnp.concatenate(pieces, axis=0).astype(BF16), NT)
        return total

    total = lax.fori_loop(0, WT // 8, scatter, jnp.zeros((48, 128), F32))

    for e in range(3):
        count = chunk_rows[e]
        rows = slice(128 * e + 128 * (e > 0), 128 * e + 128 * (e > 0) + count)
        arrived(r1.at[:, :, pl.ds(rows.start, count)], R_RS1 + e)
        for p in range(2):
            value = pay[p, span(chunk_at[e] + count * major[p], count), :].astype(F32)
            for d in range(3):
                value = value + r1[p, d, rows, :].astype(F32)
            s1[p, rows, :] = value.astype(BF16)
    for d in RING4:
        for p in range(2):
            to = (minor[p] + d) % 4
            send(s1.at[p, span(128 * to, 128)], r2.at[p, d - 1], RS2, R_RS2 + p, at_minor[p](to))

    arrived(gn_recv, PAIR + 3)
    grad_normed = grad_normed + gn_recv[...]
    standard = std[...]
    grad_gain = jnp.sum(grad_normed * standard, axis=0, keepdims=True)
    grad_hat = grad_normed * gain_ref[...]
    grad_in = istd[...] * (
        grad_hat
        - jnp.mean(grad_hat, axis=-1, keepdims=True)
        - standard * jnp.mean(grad_hat * standard, axis=-1, keepdims=True)
    )
    back_send[...] = grad_in.astype(BF16).reshape(6, 12, 2, FEAT)
    returns = (
        ((3, 6), (0, 0), (east, north)),
        ((0, 6), (3, 0), (east, lat)),
        ((3, 0), (0, 6), (lon, north)),
    )
    for source, target, device in returns:
        send(
            back_send.at[pl.ds(source[0], 3), pl.ds(source[1], 6)],
            back_recv.at[pl.ds(target[0], 3), pl.ds(target[1], 6)],
            BACK, R_BACK, device,
        )
    ginf[...] = grad_in.reshape(6, 12, 2, FEAT)

    for p in range(2):
        arrived(r2.at[p], R_RS2 + p)
        value = s1[p, span(128 * minor[p], 128), :].astype(F32)
        for d in range(3):
            value = value + r2[p, d].astype(F32)
        s2[p] = value.astype(BF16)
    for d in RING8:
        to = (z + d) % 8
        send(s2.at[:, span(16 * to, 16)], r3.at[d - 1], RS3, R_RS3, at_z(to))

    turned = total.T
    upper_part = turned.astype(BF16)
    lower_part = (turned - upper_part.astype(F32)).astype(BF16)
    spread = (iota((48, 768), 1) // 16 == iota((48, 768), 0)).astype(F32).astype(BF16)
    wide = mm(upper_part, spread) + mm(lower_part, spread)
    wide = jnp.where(iota((128, 768), 1) % 16 == iota((128, 768), 0) % 16, wide, 0.0)
    wide = jnp.sum(wide.reshape(8, 16, 768), axis=1)
    tb[...] = jnp.zeros((64, 128), F32)
    for c in range(6):
        tb[8 * c:8 * c + 8, :] = wide[:, 128 * c:128 * c + 128]
    for c in range(4):
        tb[48 + c:49 + c, :] = grad_gain[:, 128 * c:128 * c + 128]
    for d in RING4:
        to = (x + d) % 4
        send(tb.at[span(16 * to, 16)], rt1.at[d - 1], TX, R_TX, at_x(to))

    arrived(r3, R_RS3)
    for p in range(2):
        value = s2[p, span(16 * z, 16), :].astype(F32)
        for d in range(7):
            value = value + r3[d, p].astype(F32)
        g1[p, span(16 * z, 16), :] = value.astype(BF16)
    mine_z = g1.at[:, span(16 * z, 16)]
    for d in RING8:
        send(mine_z, mine_z, AG1, R_AG1, at_z((z + d) % 8))

    arrived(rt1, R_TX)
    value = tb[span(16 * x, 16), :]
    for d in range(3):
        value = value + rt1[d]
    t2[...] = value
    for d in RING4:
        send(t2, rt2.at[d - 1], TY, R_TY, at_y((y + d) % 4))

    base1 = [512 * major[p] for p in range(2)]
    base2 = [base1[p] + 128 * minor[p] for p in range(2)]
    arrived(pay.at[0, pl.ds(0, 224)], R_AG1)
    into2 = {1: R_AG2, 3: R_AG2 + 1, 2: R_AG2 + 2}
    into3 = {1: [R_AG3] * 4, 3: [R_AG3 + 1] * 4, 2: [R_AG3 + 2, R_AG3 + 3, R_AG3 + 4, R_AG3 + 5]}

    def spread_major(p, e):
        rows = span(base1[p] + 128 * ((minor[p] + 4 - e) % 4), 128)
        part = big_ref.at[core, p, rows]
        for d in RING4:
            send(g1.at[p] if e == 0 else part, part, AG3, into3[d][e], at_major[p]((major[p] + d) % 4))

    for d in RING4:
        for p in range(2):
            send(g1.at[p], big_ref.at[core, p, span(base2[p], 128)], AG2, into2[d], at_minor[p]((minor[p] + d) % 4))
    for p in range(2):
        spread_major(p, 0)
    for p in range(2):
        big_ref[core, p, span(base2[p], 128), :] = g1[p]

    arrived(rt2, R_TY)
    value = t2[...]
    for d in range(3):
        value = value + rt2[d]
    t3[...] = value
    for d in RING8:
        send(t3, rt3.at[d - 1], TZ, R_TZ, at_z((z + d) % 8))

    def forward(p, row, count):
        part = big_ref.at[core, p, span(row, count)]
        send(part, part, SIB, R_SIB, sibling)

    for e in (1, 3, 2):
        arrived(g1, into2[e])
        for p in range(2):
            spread_major(p, e)
    for p in range(2):
        forward(p, base1[p], 512)

    arrived(back_recv.at[:, three], R_BACK)
    gin_ref[0:3, 0:6] = back_recv[0:3, 0:6].astype(F32)
    gin_ref[0:3, 6:12] = back_recv[0:3, 6:12].astype(F32)
    gin_ref[3:6, 0:6] = back_recv[3:6, 0:6].astype(F32)
    gin_ref[3:6, 6:12] = ginf[0:3, 0:6]

    arrived(rt3, R_TZ)
    value = t3[...]
    for d in range(7):
        value = value + rt3[d]
    mine_t = tf.at[span(16 * x, 16)]
    mine_t[...] = value * GRAD_SCALE
    for d in RING4:
        send(mine_t, mine_t, TXG, R_TXG, at_x((x + d) % 4))

    left(xw.at[:, three], XS)
    left(cw.at[:, three], COTS)
    for n in range(3):
        left(pads.at[n], PADS + n)
    left(nrm.at[1], PAIR)
    left(validb.at[1], PAIR + 1)
    left(cotf.at[1], PAIR + 2)
    left(gn_recv, PAIR + 3)
    for e in range(3):
        left(pay.at[0, pl.ds(0, 6 * chunk_rows[e])], RS1 + e)
    left(pay.at[0, pl.ds(0, 768)], RS2)
    left(r3, RS3)
    left(pay.at[0, pl.ds(0, 224)], AG1)
    left(rt1, TX)
    left(rt2, TY)
    left(rt3, TZ)
    left(back_recv.at[:, three], BACK)

    for d in (1, 3):
        arrived(pay.at[0, pl.ds(0, 1024)], into3[d][0])
        for p in range(2):
            forward(p, 512 * ((major[p] + 4 - d) % 4), 512)
        if d == 1:
            arrived(rt1, R_TXG)
            send(tf, tf_recv, TSIB, R_TSIB, sibling)
    for e in (0, 1, 3, 2):
        arrived(g1, into3[2][e])
        for p in range(2):
            forward(p, 512 * ((major[p] + 2) % 4) + 128 * ((minor[p] + 4 - e) % 4), 128)
    left(pay.at[0, pl.ds(0, 768)], AG2)
    left(pay.at[:, pl.ds(0, 1536)], AG3)
    left(rt1, TXG)

    arrived(tf_recv, R_TSIB)
    left(tf, TSIB)
    for half, at in ((tf, core), (tf_recv, 1 - core)):
        rows = pl.ds(pl.multiple_of(8 * at, 8), 8)
        for c in range(5):
            table_ref[rows, 128 * c:128 * c + 128] = half[8 * c:8 * c + 8, :]
        table_ref[rows, 640:NBIAS] = half[40:48, 0:NBIAS - 640]
    for c in range(4):
        ggain_ref[:, 128 * c:128 * c + 128] = tf[48 + c:49 + c, :] + tf_recv[48 + c:49 + c, :]

    arrived(big_ref.at[1 - core], R_SIB)
    left(pay, SIB)


def widen(big, gin, table, gain, gin_out, gain_out, wqkv_out, wout_out, table_out, wqkv, wout, sem):
    made = [
        pltpu.make_async_copy(gin, gin_out, sem.at[0]),
        pltpu.make_async_copy(gain, gain_out, sem.at[1]),
        pltpu.make_async_copy(table, table_out, sem.at[2]),
    ]
    for one in made:
        one.start()
    for step in range(4):
        rows = slice(128 * step, 128 * step + 128)
        for block in range(3):
            start = (512 * step + 384, 512 * step + 256, 512 * (step // 2) + 128 * (step % 2))[block]
            for core in range(2):
                for p in range(2):
                    lanes = slice(512 * block + 256 * core + 128 * p, 512 * block + 256 * core + 128 * p + 128)
                    wqkv[rows, lanes] = big[core, p, start:start + 128, :].astype(F32) * GRAD_SCALE
        one = pltpu.make_async_copy(wqkv.at[pl.ds(128 * step, 128)], wqkv_out.at[pl.ds(128 * step, 128)], sem.at[3 + step])
        one.start()
        made.append(one)
        core, half = step // 2, step % 2
        for p in range(2):
            for u in range(2):
                start = 1024 + 512 * u + 128 * half
                lanes = slice(256 * p + 128 * u, 256 * p + 128 * u + 128)
                wout[rows, lanes] = big[core, p, start:start + 128, :].astype(F32) * GRAD_SCALE
        one = pltpu.make_async_copy(wout.at[pl.ds(128 * step, 128)], wout_out.at[pl.ds(128 * step, 128)], sem.at[7 + step])
        one.start()
        made.append(one)
    for one in made:
        one.wait()


def per_device(inputs, cotangent, pad_mask, rel_index, bias_table, ln_gain, w_qkv, w_out):
    vmem = pl.BlockSpec(memory_space=pltpu.VMEM)
    hbm = pl.BlockSpec(memory_space=pltpu.HBM)
    big, grad_in, table, gain = pl.pallas_call(
        body,
        out_shape=(
            jax.ShapeDtypeStruct((2, 2, 2048, 128), BF16),
            jax.ShapeDtypeStruct((6, 12, 2, FEAT), F32),
            jax.ShapeDtypeStruct((HEADS, NBIAS), F32),
            jax.ShapeDtypeStruct((1, FEAT), F32),
        ),
        in_specs=[hbm] * 8,
        out_specs=[vmem] * 4,
        scratch_shapes=[
            pltpu.VMEM((6, 12), I32),
            pltpu.VMEM((WT, WT), I32),
            pltpu.VMEM((8, NBIAS), F32),
            pltpu.VMEM((1, FEAT), F32),
            pltpu.VMEM((FEAT, 768), BF16),
            pltpu.VMEM((256, FEAT), BF16),
            pltpu.VMEM((768, FEAT), BF16),
            pltpu.VMEM((FEAT, 256), BF16),
            pltpu.VMEM((6, 12, 2, FEAT), BF16),
            pltpu.VMEM((6, 12, 2, FEAT), BF16),
            pltpu.VMEM((3, 6, 12), I32),
            pltpu.VMEM((32, 128), F32),
            pltpu.VMEM((WT, 256), I32),
            pltpu.VMEM((8, 1, 768), F32),
            pltpu.VMEM((2, 16, 128), I32),
            pltpu.VMEM((8, 2, 16, 128), F32),
            pltpu.VMEM((8, WT, WT), F32),
            pltpu.VMEM((2, WT, 128), BF16),
            pltpu.VMEM((2, WT, WT), F32),
            pltpu.VMEM((WT, FEAT), F32),
            pltpu.VMEM((WT, 1), F32),
            pltpu.VMEM((2, WT, FEAT), BF16),
            pltpu.VMEM((2, FEAT, WT), BF16),
            pltpu.VMEM((2, WT, FEAT), BF16),
            pltpu.VMEM((2, WT, 768), BF16),
            pltpu.VMEM((2, 768, WT), BF16),
            pltpu.VMEM((2, WT, 256), BF16),
            pltpu.VMEM((2, 256, WT), BF16),
            pltpu.VMEM((2, 256, WT), BF16),
            pltpu.VMEM((2, 256, WT), BF16),
            pltpu.VMEM((2, WT, 768), BF16),
            pltpu.VMEM((2, 8, WT, WT), F32),
            pltpu.VMEM((8, WT, WT), F32),
            pltpu.VMEM((WT, FEAT), F32),
            pltpu.VMEM((WT, FEAT), F32),
            pltpu.VMEM((2, 2048, 128), BF16),
            pltpu.VMEM((2, 3, 512, 128), BF16),
            pltpu.VMEM((2, 512, 128), BF16),
            pltpu.VMEM((2, 3, 128, 128), BF16),
            pltpu.VMEM((2, 128, 128), BF16),
            pltpu.VMEM((7, 2, 16, 128), BF16),
            pltpu.VMEM((2, 128, 128), BF16),
            pltpu.VMEM((64, 128), F32),
            pltpu.VMEM((3, 16, 128), F32),
            pltpu.VMEM((16, 128), F32),
            pltpu.VMEM((3, 16, 128), F32),
            pltpu.VMEM((16, 128), F32),
            pltpu.VMEM((7, 16, 128), F32),
            pltpu.VMEM((64, 128), F32),
            pltpu.VMEM((64, 128), F32),
            pltpu.VMEM((6, 12, 2, FEAT), BF16),
            pltpu.VMEM((6, 12, 2, FEAT), BF16),
            pltpu.VMEM((6, 12, 2, FEAT), F32),
            pltpu.SemaphoreType.DMA((SENDS,)),
            pltpu.SemaphoreType.DMA((RECVS,)),
            pltpu.SemaphoreType.DMA((10,)),
        ],
        compiler_params=pltpu.CompilerParams(
            collective_id=0, has_side_effects=True, vmem_limit_bytes=48 * 1024 * 1024
        ),
    )(
        *(
            pltpu.with_memory_space_constraint(one, pltpu.HBM)
            for one in (
                inputs.transpose(1, 2, 0, 3),
                cotangent.transpose(1, 2, 0, 3),
                pad_mask,
                rel_index,
                bias_table.T,
                ln_gain.reshape(1, FEAT),
                w_qkv,
                w_out,
            )
        )
    )
    grad_in, gain, wqkv, wout, table = pl.pallas_call(
        widen,
        out_shape=(
            jax.ShapeDtypeStruct((6, 12, 2, FEAT), F32),
            jax.ShapeDtypeStruct((1, FEAT), F32),
            jax.ShapeDtypeStruct((FEAT, 3 * FEAT), F32),
            jax.ShapeDtypeStruct((FEAT, FEAT), F32),
            jax.ShapeDtypeStruct((HEADS, NBIAS), F32),
        ),
        in_specs=[vmem] * 4,
        out_specs=[hbm] * 5,
        scratch_shapes=[
            pltpu.VMEM((FEAT, 3 * FEAT), F32),
            pltpu.VMEM((FEAT, FEAT), F32),
            pltpu.SemaphoreType.DMA((11,)),
        ],
        compiler_params=pltpu.CompilerParams(vmem_limit_bytes=24 * 1024 * 1024),
    )(big, grad_in, table, gain)
    return grad_in.transpose(2, 0, 1, 3), gain.reshape(FEAT), wqkv, wout, table.T


def solution(mesh):
    in_specs = (
        P(None, "lat", "lon", None),
        P(None, "lat", "lon", None),
        P("lat", "lon"),
        P(),
        P(),
        P(),
        P(),
        P(),
    )
    out_specs = (P(None, "lat", "lon", None), P(), P(), P(), P())
    return jax.shard_map(
        per_device, mesh=mesh, in_specs=in_specs, out_specs=out_specs, check_vma=False
    )
```

time: 68.7 us -> 63.7 us (0.927)
  Pallas kernels: 68 us -> 63 us
    pallas_call x1, Pallas kernels: 65.8 us -> 60.8 us  [per_device(): pl.pallas_call(body, out_shape=(jax.ShapeDtypeStruct((2, 2, 2048, 128), B...]
where the time goes in v3:
time: 63.7 us
  Pallas kernels  63 us (99%)
  between operations  0.64 us (1%)
    pallas_call x1, Pallas kernels, per_device(): pl.pallas_call(body, out_shape=(jax.ShapeDtypeStruct((2, 2, 2048, 128), B...  60.8 us
    pallas_call x1, Pallas kernels, per_device(): pl.pallas_call(widen, out_shape=(jax.ShapeDtypeStruct((6, 12, 2, FEAT), F...  2.21 us

profile of v3, /device:TPU:1, one launch (start us, length us, event | category | flops | bytes accessed | tf_op | source)
XLA Modules:
  0.0 63.7 jit_solution(14830424915789995865)
XLA Ops:
  0.6 60.8 %shard_map.119 = (bf16[2,2,2048,128]{3,2,1,0:T(8,128)(2,1)S(1)}, f32[6,12,2,512]{3,2,1,0:T(2,128)S(1)}, f32[16,759]{1,0:T(8,128)S(1)}, f32[1,512]{1,0:T(1,128)S(1)}) custom-call(bf16[6,12,2,512]{3,2,1,0:T(2,128)(2,1)} %bitcast.7, bf16[6,12,2,512]{3,2,1,0:T(2,128)(2,1)} %bitcast.8, s32[6,12]{1,0:T(8,128)} %pad_hbm.1, s32[144,144]{1,0:T(8,128)} %rel_hbm.1, ...), custom_call_target="tpu_custom_call" | custom-call | tf_op jit(solution)/shard_map/pallas_call | solution.py:599
  61.5 2.2 %shard_map.120 = (f32[6,12,2,512]{3,2,1,0:T(2,128)}, f32[1,512]{1,0:T(1,128)}, f32[512,1536]{1,0:T(8,128)}, f32[512,512]{1,0:T(8,128)}, f32[16,759]{1,0:T(8,128)}) custom-call(bf16[2,2,2048,128]{3,2,1,0:T(8,128)(2,1)S(1)} %get-tuple-element.14.big, f32[6,12,2,512]{3,2,1,0:T(2,128)S(1)} %get-tuple-element.15.gin, f32[16,759]{1,0:T(8,128)S(1)} %get-tuple-element.16.table, ...), custom_call_target="tpu_custom_call" | custom-call | tf_op jit(solution)/shard_map/pallas_call | solution.py:685

commit v4 on v3

--- a/solution.py
+++ b/solution.py
@@ -46,8 +46,8 @@
     x_ref, cot_ref, pad_hbm, rel_hbm, bias_hbm, gain_hbm, wqkv_hbm, wout_hbm,
     big_ref, gin_ref, table_ref, ggain_ref,
     pad_ref, rel_ref, bias_ref, gain_ref, wq, wo, wqt, wot,
-    xw, cw, pads, padf, relt, tab, edge, edge_bias, bias, validb, allow, std, istd, nrm, nrmt, cotf,
-    proj, projt, gatt, gattt, attt, gradt, gnat, probs, ds, gn_send, gn_recv,
+    xw, cw, pads, padf, relt, tab, edge_row, edge, edge_bias, bias, bias_rest, validb, allow, allow_rest, std, istd, nrm, nrmt, cotf,
+    proj, projt, gatt, gattt, attt, gradt, gnat, probs, probs_rest, values_rest, ds, ds_rest, gn_send, gn_recv,
     pay, r1, s1, r2, s2, r3, g1,
     tb, rt1, t2, rt2, t3, rt3, tf, tf_recv,
     back_send, back_recv, ginf, ssem, rsem, lsem,
@@ -141,8 +141,13 @@
     rel = rel_ref[...]
     low = mm(mm(order, (rel & 255).astype(F32).astype(BF16), NT).astype(BF16), order, NT)
     high = mm(mm(order, (rel >> 8).astype(F32).astype(BF16), NT).astype(BF16), order, NT)
-    relt[...] = jnp.zeros((WT, 256), I32)
-    relt[:, :WT] = (high * 256.0 + low).astype(I32)
+    index = (high * 256.0 + low).astype(I32)
+    relt[...] = index[:, 0:128]
+    edge_row[...] = jnp.zeros((16, 256), I32)
+    edge_row[:, 0:WT] = index.T[128:WT, :]
+    ds_rest[...] = jnp.zeros((256, 128), F32)
+    edge[0] = edge_row[:, 0:128]
+    edge[1] = edge_row[:, 128:256]
     tab[...] = jnp.zeros((8, 1, 768), F32)
     for head in range(8):
         tab[head, :, :NBIAS] = bias_ref[head:head + 1, :]
@@ -162,29 +167,28 @@
         rows = pl.ds(pl.multiple_of(8 * step, 8), 8)
 
         def put(head, found):
-            bias[head, rows, 0:128] = found
-
-        gather_heads(relt[rows, 0:128], put)
+            bias[head, rows, :] = found
+
+        gather_heads(relt[rows, :], put)
         return carry
 
     lax.fori_loop(0, WT // 8, lookup, 0)
-    rest_index = relt[:, 128:256].T
-    edge[0] = rest_index[0:16, 0:128]
-    edge[1] = jnp.concatenate([rest_index[0:16, 128:WT], jnp.zeros((16, 256 - WT), I32)], axis=1)
-
     def lookup_rest(step, carry):
         part, half = step // 2, pl.ds(pl.multiple_of(8 * (step % 2), 8), 8)
 
         def put(head, found):
-            edge_bias[head, part, half, :] = found
+            edge_bias[part, pl.ds(pl.multiple_of(16 * head + 8 * (step % 2), 8), 8), :] = found
 
         gather_heads(edge[part, half, :], put)
         return carry
 
     lax.fori_loop(0, 4, lookup_rest, 0)
-    for head in range(8):
-        bias[head, 0:128, 128:WT] = edge_bias[head, 0].T
-        bias[head, 128:WT, 128:WT] = edge_bias[head, 1].T[0:16, :]
+    bias_rest[0:128, :] = edge_bias[0].T
+    bias_rest[128:WT, :] = edge_bias[1].T[0:16, :]
+    deal = ((iota((WT, 128), 0) - 128) == iota((WT, 128), 1) % 16).astype(F32).astype(BF16)
+    gather_up = (iota((128, WT), 0) % 16 == (iota((128, WT), 1) - 128)).astype(F32).astype(BF16)
+    own_rows = (iota((256, 128), 0) // HEAD_SIZE == iota((256, 128), 1) // 16).astype(F32)
+    own_cols = (iota((128, 256), 0) // 16 == iota((128, 256), 1) // HEAD_SIZE).astype(F32)
 
     for name in ("wo", "wq0", "wq1", "wq2", "pad", "x", "cot", "gain"):
         loads[name].wait()
@@ -235,7 +239,9 @@
         across = lat + w * (1 - 2 * core) == 15
         same_group = ((key >= 72) == (query >= 72)) | jnp.logical_not(across)
         valid_key = validb[w].astype(F32)[:, 0:1] > 0.5
-        allow[w] = (same_group & (valid_key | (key == query))).astype(F32)
+        seen = (same_group & (valid_key | (key == query))).astype(F32)
+        allow[w] = seen[:, 0:128]
+        allow_rest[w] = mm(seen.astype(BF16), deal)
 
     see(0)
     arrived(cw.at[:, three], COTS)
@@ -248,61 +254,81 @@
 
     project_cot(0)
 
-    def picks(group):
-        lanes = [pl.ds(pl.multiple_of(256 * b + group * 128, 128), 128) for b in range(3)]
-        head_of_lane = iota((1, 128), 1) // HEAD_SIZE
-        mine = [(head_of_lane == j).astype(F32).astype(BF16) for j in range(4)]
-        return lanes, mine
-
-    def rows_of(head):
-        return [pl.ds(pl.multiple_of(256 * b + head * HEAD_SIZE, HEAD_SIZE), HEAD_SIZE) for b in range(3)]
+    lane_head = iota((1, 128), 1) // HEAD_SIZE
+    mine = [(lane_head == j).astype(F32).astype(BF16) for j in range(4)]
+
+    def apart(group):
+        return jnp.concatenate([group * mine[j] for j in range(4)], axis=0)
+
+    def own_blocks(wide):
+        return [wide[32 * j:32 * j + 32, 128 * j:128 * j + 128].astype(BF16) for j in range(4)]
+
+    def softmax(scores, seen, added):
+        scores = jnp.where(seen > 0.5, scores * SCORE_SCALE + added, MASKED)
+        exponent = jnp.exp(scores - jnp.max(scores, axis=0, keepdims=True))
+        return exponent * (1.0 / jnp.sum(exponent, axis=0, keepdims=True))
+
+    def softmax_grad(prob, grad_probs):
+        return prob * (grad_probs - jnp.sum(prob * grad_probs, axis=0, keepdims=True))
+
+    def fold(wide):
+        return mm((wide * own_rows).astype(BF16), gather_up)[:, 128:WT].astype(BF16)
 
     def forward_heads(w):
-        def step(group, carry):
-            lanes, mine = picks(group)
-            k_group, ga_group = proj[w, :, lanes[1]], gatt[w, :, lanes[0]]
-            qt_group = projt[w, span(128 * group, 128), :]
-            grad_values = jnp.zeros((WT, 128), F32)
+        rest_queries = (mm(projt[w, 0:256, :], deal) * own_rows).astype(BF16)
+        prob = softmax(mm(proj[w, :, 256:512], rest_queries), allow_rest[w], bias_rest[...])
+        probs_rest[w] = prob
+        prob_b = prob.astype(BF16)
+        attt[w, :, 128:WT] = fold(mm(projt[w, 512:768, :], prob_b))
+        rest_cot = (mm(gather_up, gatt[w]) * own_cols).astype(BF16)
+        values_rest[...] = mm(prob_b, rest_cot)
+
+        for group in range(2):
+            here = slice(128 * group, 128 * group + 128)
+            keys_at, values_at = slice(256 + here.start, 256 + here.stop), slice(512 + here.start, 512 + here.stop)
+            scores = mm(apart(proj[w, :, keys_at]), projt[w, here, 0:128])
+            four = []
             for j in range(4):
                 head = group * 4 + j
-                rows = rows_of(head)
-                scores = mm(k_group * mine[j], qt_group) * SCORE_SCALE
-                scores = jnp.where(allow[w] > 0.5, scores + bias[head], MASKED)
-                exponent = jnp.exp(scores - jnp.max(scores, axis=0, keepdims=True))
-                prob = exponent * (1.0 / jnp.sum(exponent, axis=0, keepdims=True))
+                prob = softmax(scores[WT * j:WT * j + WT], allow[w], bias[head])
                 probs[w, head] = prob
-                prob_b = prob.astype(BF16)
-                attt[w, rows[0], :] = mm(projt[w, rows[2], :], prob_b).astype(BF16)
-                grad_values = grad_values + mm(prob_b, ga_group * mine[j])
-            gnat[w, :, lanes[2]] = grad_values.astype(BF16)
-            return carry
-
-        lax.fori_loop(0, 2, step, 0)
+                four.append(prob.astype(BF16))
+            four = jnp.concatenate(four, axis=1)
+            for j, block in enumerate(own_blocks(mm(projt[w, values_at, :], four))):
+                attt[w, 32 * (4 * group + j):32 * (4 * group + j) + 32, 0:128] = block
+            grad_values = values_rest[:, here] + mm(four, apart(gatt[w, 0:128, here]))
+            gnat[w, :, values_at] = grad_values.astype(BF16)
 
     def backward_heads(w):
-        def step(group, carry):
-            lanes, mine = picks(group)
-            q_group, v_group = proj[w, :, lanes[0]], proj[w, :, lanes[2]]
-            gat_group = gattt[w, span(128 * group, 128), :]
-            grad_keys = jnp.zeros((WT, 128), F32)
+        rest_cot = (mm(gattt[w], deal) * own_rows).astype(BF16)
+        grad_scores = softmax_grad(probs_rest[w], mm(proj[w, :, 512:768], rest_cot))
+        if w == 0:
+            ds_rest[0:WT, :] = grad_scores
+        else:
+            ds_rest[0:WT, :] = ds_rest[0:WT, :] + grad_scores
+        grad_b = grad_scores.astype(BF16)
+        gradt[w, :, 128:WT] = fold(mm(projt[w, 256:512, :], grad_b) * SCORE_SCALE)
+        rest_queries = (mm(gather_up, proj[w, :, 0:256]) * own_cols).astype(BF16)
+        values_rest[...] = mm(grad_b, rest_queries)
+
+        for group in range(2):
+            here = slice(128 * group, 128 * group + 128)
+            keys_at, values_at = slice(256 + here.start, 256 + here.stop), slice(512 + here.start, 512 + here.stop)
+            grad_probs = mm(apart(proj[w, :, values_at]), gattt[w, here, 0:128])
+            four = []
             for j in range(4):
                 head = group * 4 + j
-                rows = rows_of(head)
-                prob = probs[w, head]
-                grad_probs = mm(v_group * mine[j], gat_group)
-                inner = jnp.sum(prob * grad_probs, axis=0, keepdims=True)
-                grad_scores = prob * (grad_probs - inner)
+                grad_scores = softmax_grad(probs[w, head], grad_probs[WT * j:WT * j + WT])
                 if w == 0:
                     ds[head] = grad_scores
                 else:
                     ds[head] = ds[head] + grad_scores
-                grad_b = grad_scores.astype(BF16)
-                gradt[w, rows[0], :] = (mm(projt[w, rows[1], :], grad_b) * SCORE_SCALE).astype(BF16)
-                grad_keys = grad_keys + mm(grad_b, q_group * mine[j])
-            gnat[w, :, lanes[1]] = (grad_keys * SCORE_SCALE).astype(BF16)
-            return carry
-
-        lax.fori_loop(0, 2, step, 0)
+                four.append(grad_scores.astype(BF16))
+            four = jnp.concatenate(four, axis=1)
+            for j, block in enumerate(own_blocks(mm(projt[w, keys_at, :], four) * SCORE_SCALE)):
+                gradt[w, 32 * (4 * group + j):32 * (4 * group + j) + 32, 0:128] = block
+            grad_keys = values_rest[:, here] + mm(four, apart(proj[w, 0:128, here]))
+            gnat[w, :, keys_at] = (grad_keys * SCORE_SCALE).astype(BF16)
 
     forward_heads(0)
     arrived(nrm.at[1], PAIR)
@@ -359,24 +385,24 @@
     send(gn_send, gn_recv, PAIR + 3, PAIR + 3, sibling)
     grad_normed = mm(gnat[0], wqt[...])
 
-    ones = iota((48, WT), 0)
-    sub = iota((16, WT), 0)
+    def table_part(pairs):
+        upper, pieces = [], []
+        for index, rows_in in pairs:
+            lanes = index.shape[1]
+            upper.append((iota((48, lanes), 0) == (index >> 4)).astype(F32).astype(BF16))
+            match = iota((16, lanes), 0) == (index & 15)
+            pieces.append(jnp.concatenate(
+                [jnp.where(match, jnp.broadcast_to(row, (16, lanes)), 0.0) for row in rows_in], axis=0
+            ).astype(BF16))
+        return mm(jnp.concatenate(pieces, axis=1), jnp.concatenate(upper, axis=1), NT)
 
     def scatter(step, total):
         rows = pl.ds(pl.multiple_of(8 * step, 8), 8)
-        indices = relt[rows, 0:WT]
-        for k in range(8):
-            index = indices[k:k + 1, :]
-            upper = (ones == (index >> 4)).astype(F32).astype(BF16)
-            match = sub == (index & 15)
-            pieces = [
-                jnp.where(match, jnp.broadcast_to(ds[h, rows, :][k:k + 1, :], (16, WT)), 0.0)
-                for h in range(8)
-            ]
-            total = total + mm(upper, jnp.concatenate(pieces, axis=0).astype(BF16), NT)
-        return total
-
-    total = lax.fori_loop(0, WT // 8, scatter, jnp.zeros((48, 128), F32))
+        indices = relt[rows, :]
+        values = [ds[h, rows, :] for h in range(8)]
+        return total + table_part([(indices[k:k + 1, :], [one[k:k + 1, :] for one in values]) for k in range(8)])
+
+    total = lax.fori_loop(0, WT // 8, scatter, jnp.zeros((128, 48), F32))
 
     for e in range(3):
         count = chunk_rows[e]
@@ -426,7 +452,13 @@
         to = (z + d) % 8
         send(s2.at[:, span(16 * to, 16)], r3.at[d - 1], RS3, R_RS3, at_z(to))
 
-    turned = total.T
+    turned_rest = ds_rest[...].T
+    turned = total
+    for half in range(2):
+        turned = turned + table_part([
+            (edge_row[n:n + 1, :], [turned_rest[16 * h + n:16 * h + n + 1, :] for h in range(8)])
+            for n in range(8 * half, 8 * half + 8)
+        ])
     upper_part = turned.astype(BF16)
     lower_part = (turned - upper_part.astype(F32)).astype(BF16)
     spread = (iota((48, 768), 1) // 16 == iota((48, 768), 0)).astype(F32).astype(BF16)
@@ -619,13 +651,16 @@
             pltpu.VMEM((6, 12, 2, FEAT), BF16),
             pltpu.VMEM((3, 6, 12), I32),
             pltpu.VMEM((32, 128), F32),
-            pltpu.VMEM((WT, 256), I32),
+            pltpu.VMEM((WT, 128), I32),
             pltpu.VMEM((8, 1, 768), F32),
+            pltpu.VMEM((16, 256), I32),
             pltpu.VMEM((2, 16, 128), I32),
-            pltpu.VMEM((8, 2, 16, 128), F32),
-            pltpu.VMEM((8, WT, WT), F32),
+            pltpu.VMEM((2, 128, 128), F32),
+            pltpu.VMEM((8, WT, 128), F32),
+            pltpu.VMEM((WT, 128), F32),
             pltpu.VMEM((2, WT, 128), BF16),
-            pltpu.VMEM((2, WT, WT), F32),
+            pltpu.VMEM((2, WT, 128), F32),
+            pltpu.VMEM((2, WT, 128), F32),
             pltpu.VMEM((WT, FEAT), F32),
             pltpu.VMEM((WT, 1), F32),
             pltpu.VMEM((2, WT, FEAT), BF16),
@@ -638,8 +673,11 @@
             pltpu.VMEM((2, 256, WT), BF16),
             pltpu.VMEM((2, 256, WT), BF16),
             pltpu.VMEM((2, WT, 768), BF16),
-            pltpu.VMEM((2, 8, WT, WT), F32),
-            pltpu.VMEM((8, WT, WT), F32),
+            pltpu.VMEM((2, 8, WT, 128), F32),
+            pltpu.VMEM((2, WT, 128), F32),
+            pltpu.VMEM((WT, 256), F32),
+            pltpu.VMEM((8, WT, 128), F32),
+            pltpu.VMEM((256, 128), F32),
             pltpu.VMEM((WT, FEAT), F32),
             pltpu.VMEM((WT, FEAT), F32),
             pltpu.VMEM((2, 2048, 128), BF16),

time: 63.7 us -> 58.6 us (0.920)
  Pallas kernels: 63 us -> 57.9 us
    pallas_call x1, Pallas kernels: 60.8 us -> 55.7 us  [per_device(): pl.pallas_call(body, out_shape=(jax.ShapeDtypeStruct((2, 2, 2048, 128), B...]
where the time goes in v4:
time: 58.6 us; the launch traced here: 58.5 us
  Pallas kernels  57.9 us (99%)
  between operations  0.64 us (1%)
    pallas_call x1, Pallas kernels, per_device(): pl.pallas_call(body, out_shape=(jax.ShapeDtypeStruct((2, 2, 2048, 128), B...  55.7 us
    pallas_call x1, Pallas kernels, per_device(): pl.pallas_call(widen, out_shape=(jax.ShapeDtypeStruct((6, 12, 2, FEAT), F...  2.21 us

profile of v4, /device:TPU:1, one launch (start us, length us, event | category | flops | bytes accessed | tf_op | source)
XLA Modules:
  0.0 58.5 jit_solution(9039610369508021549)
XLA Ops:
  0.6 55.7 %shard_map.119 = (bf16[2,2,2048,128]{3,2,1,0:T(8,128)(2,1)S(1)}, f32[6,12,2,512]{3,2,1,0:T(2,128)S(1)}, f32[16,759]{1,0:T(8,128)S(1)}, f32[1,512]{1,0:T(1,128)S(1)}) custom-call(bf16[6,12,2,512]{3,2,1,0:T(2,128)(2,1)} %bitcast.7, bf16[6,12,2,512]{3,2,1,0:T(2,128)(2,1)} %bitcast.8, s32[6,12]{1,0:T(8,128)} %pad_hbm.1, s32[144,144]{1,0:T(8,128)} %rel_hbm.1, ...), custom_call_target="tpu_custom_call" | custom-call | tf_op jit(solution)/shard_map/pallas_call | solution.py:631
  56.3 2.2 %shard_map.120 = (f32[6,12,2,512]{3,2,1,0:T(2,128)}, f32[1,512]{1,0:T(1,128)}, f32[512,1536]{1,0:T(8,128)}, f32[512,512]{1,0:T(8,128)}, f32[16,759]{1,0:T(8,128)}) custom-call(bf16[2,2,2048,128]{3,2,1,0:T(8,128)(2,1)S(1)} %get-tuple-element.14.big, f32[6,12,2,512]{3,2,1,0:T(2,128)S(1)} %get-tuple-element.15.gin, f32[16,759]{1,0:T(8,128)S(1)} %get-tuple-element.16.table, ...), custom_call_target="tpu_custom_call" | custom-call | tf_op jit(solution)/shard_map/pallas_call | solution.py:723

commit v5 on v4

--- a/solution.py
+++ b/solution.py
@@ -26,9 +26,9 @@
 XS, COTS, PADS, PAIR, RS1, RS2, RS3, AG1, AG2, AG3, SIB = 0, 1, 2, 5, 9, 12, 13, 14, 15, 16, 17
 TX, TY, TZ, TXG, TSIB, BACK = 18, 19, 20, 21, 22, 23
 SENDS = 24
-R_RS1, R_RS2, R_RS3, R_AG1, R_AG2, R_AG3, R_SIB = 9, 12, 14, 15, 16, 19, 25
-R_TX, R_TY, R_TZ, R_TXG, R_TSIB, R_BACK = 26, 27, 28, 29, 30, 31
-RECVS = 32
+R_RS1, R_RS2, R_RS3, R_AG1, R_AG2, R_AG3, R_SIB = 9, 12, 14, 15, 16, 19, 23
+R_TX, R_TY, R_TZ, R_TXG, R_TSIB, R_BACK = 24, 25, 26, 27, 28, 29
+RECVS = 30
 
 RING4 = (2, 1, 3)
 RING8 = (4, 3, 5, 2, 6, 1, 7)
@@ -47,7 +47,7 @@
     big_ref, gin_ref, table_ref, ggain_ref,
     pad_ref, rel_ref, bias_ref, gain_ref, wq, wo, wqt, wot,
     xw, cw, pads, padf, relt, tab, edge_row, edge, edge_bias, bias, bias_rest, validb, allow, allow_rest, std, istd, nrm, nrmt, cotf,
-    proj, projt, gatt, gattt, attt, gradt, gnat, probs, probs_rest, values_rest, ds, ds_rest, gn_send, gn_recv,
+    proj, projt, gatt, gattt, attt, gradt, gnat, probs, probs_rest, keys_rest, probs_b, ds, ds_rest, gn_send, gn_recv,
     pay, r1, s1, r2, s2, r3, g1,
     tb, rt1, t2, rt2, t3, rt3, tf, tf_recv,
     back_send, back_recv, ginf, ssem, rsem, lsem,
@@ -193,8 +193,8 @@
     for name in ("wo", "wq0", "wq1", "wq2", "pad", "x", "cot", "gain"):
         loads[name].wait()
     wot[...] = wo[...].T
-    for block in range(3):
-        wqt[256 * block:256 * block + 256, :] = wq[:, 256 * block:256 * block + 256].T
+    for block, start in enumerate((256, 0, 384, 128, 512, 640)):
+        wqt[128 * block:128 * block + 128, :] = wq[:, start:start + 128].T
 
     arrived(xw.at[:, three], XS)
     tokens = xw[...].astype(F32).reshape(WT, FEAT)
@@ -244,15 +244,10 @@
         allow_rest[w] = mm(seen.astype(BF16), deal)
 
     see(0)
-    arrived(cw.at[:, three], COTS)
-    cotf[0] = cw[...].reshape(WT, FEAT)
-    send(cotf.at[0], cotf.at[1], PAIR + 2, PAIR + 2, sibling)
 
     def project_cot(w):
         gatt[w] = mm(cotf[w], wot[...]).astype(BF16)
         gattt[w] = gatt[w].T
-
-    project_cot(0)
 
     lane_head = iota((1, 128), 1) // HEAD_SIZE
     mine = [(lane_head == j).astype(F32).astype(BF16) for j in range(4)]
@@ -274,14 +269,11 @@
     def fold(wide):
         return mm((wide * own_rows).astype(BF16), gather_up)[:, 128:WT].astype(BF16)
 
-    def forward_heads(w):
+    def attend(w):
         rest_queries = (mm(projt[w, 0:256, :], deal) * own_rows).astype(BF16)
         prob = softmax(mm(proj[w, :, 256:512], rest_queries), allow_rest[w], bias_rest[...])
         probs_rest[w] = prob
-        prob_b = prob.astype(BF16)
-        attt[w, :, 128:WT] = fold(mm(projt[w, 512:768, :], prob_b))
-        rest_cot = (mm(gather_up, gatt[w]) * own_cols).astype(BF16)
-        values_rest[...] = mm(prob_b, rest_cot)
+        attt[w, :, 128:WT] = fold(mm(projt[w, 512:768, :], prob.astype(BF16)))
 
         for group in range(2):
             here = slice(128 * group, 128 * group + 128)
@@ -296,10 +288,17 @@
             four = jnp.concatenate(four, axis=1)
             for j, block in enumerate(own_blocks(mm(projt[w, values_at, :], four))):
                 attt[w, 32 * (4 * group + j):32 * (4 * group + j) + 32, 0:128] = block
-            grad_values = values_rest[:, here] + mm(four, apart(gatt[w, 0:128, here]))
-            gnat[w, :, values_at] = grad_values.astype(BF16)
-
-    def backward_heads(w):
+            probs_b[w, group] = four
+
+    def values_grad(w):
+        rest_cot = (mm(gather_up, gatt[w]) * own_cols).astype(BF16)
+        rest = mm(probs_rest[w].astype(BF16), rest_cot)
+        for group in range(2):
+            here = slice(128 * group, 128 * group + 128)
+            grad_values = rest[:, here] + mm(probs_b[w, group], apart(gatt[w, 0:128, here]))
+            gnat[w, :, 512 + here.start:512 + here.stop] = grad_values.astype(BF16)
+
+    def backward_rest(w):
         rest_cot = (mm(gattt[w], deal) * own_rows).astype(BF16)
         grad_scores = softmax_grad(probs_rest[w], mm(proj[w, :, 512:768], rest_cot))
         if w == 0:
@@ -309,43 +308,49 @@
         grad_b = grad_scores.astype(BF16)
         gradt[w, :, 128:WT] = fold(mm(projt[w, 256:512, :], grad_b) * SCORE_SCALE)
         rest_queries = (mm(gather_up, proj[w, :, 0:256]) * own_cols).astype(BF16)
-        values_rest[...] = mm(grad_b, rest_queries)
-
-        for group in range(2):
-            here = slice(128 * group, 128 * group + 128)
-            keys_at, values_at = slice(256 + here.start, 256 + here.stop), slice(512 + here.start, 512 + here.stop)
-            grad_probs = mm(apart(proj[w, :, values_at]), gattt[w, here, 0:128])
-            four = []
-            for j in range(4):
-                head = group * 4 + j
-                grad_scores = softmax_grad(probs[w, head], grad_probs[WT * j:WT * j + WT])
-                if w == 0:
-                    ds[head] = grad_scores
-                else:
-                    ds[head] = ds[head] + grad_scores
-                four.append(grad_scores.astype(BF16))
-            four = jnp.concatenate(four, axis=1)
-            for j, block in enumerate(own_blocks(mm(projt[w, keys_at, :], four) * SCORE_SCALE)):
-                gradt[w, 32 * (4 * group + j):32 * (4 * group + j) + 32, 0:128] = block
-            grad_keys = values_rest[:, here] + mm(four, apart(proj[w, 0:128, here]))
-            gnat[w, :, keys_at] = (grad_keys * SCORE_SCALE).astype(BF16)
-
-    forward_heads(0)
+        keys_rest[w] = mm(grad_b, rest_queries)
+
+    def backward_group(w, group):
+        here = slice(128 * group, 128 * group + 128)
+        keys_at, values_at = slice(256 + here.start, 256 + here.stop), slice(512 + here.start, 512 + here.stop)
+        grad_probs = mm(apart(proj[w, :, values_at]), gattt[w, here, 0:128])
+        four = []
+        for j in range(4):
+            head = group * 4 + j
+            grad_scores = softmax_grad(probs[w, head], grad_probs[WT * j:WT * j + WT])
+            if w == 0:
+                ds[head] = grad_scores
+            else:
+                ds[head] = ds[head] + grad_scores
+            four.append(grad_scores.astype(BF16))
+        four = jnp.concatenate(four, axis=1)
+        for j, block in enumerate(own_blocks(mm(projt[w, keys_at, :], four) * SCORE_SCALE)):
+            gradt[w, 32 * (4 * group + j):32 * (4 * group + j) + 32, 0:128] = block
+        grad_keys = keys_rest[w, :, here] + mm(four, apart(proj[w, 0:128, here]))
+        gnat[w, :, 256 * group:256 * group + 128] = (grad_keys * SCORE_SCALE).astype(BF16)
+        gnat[w, :, 256 * group + 128:256 * group + 256] = gradt[w, here, :].T
+
+    attend(0)
+    arrived(cw.at[:, three], COTS)
+    cotf[0] = cw[...].reshape(WT, FEAT)
+    send(cotf.at[0], cotf.at[1], PAIR + 2, PAIR + 2, sibling)
+    project_cot(0)
     arrived(nrm.at[1], PAIR)
     project(1)
     arrived(validb.at[1], PAIR + 1)
     see(1)
+    attend(1)
+    values_grad(0)
     arrived(cotf.at[1], PAIR + 2)
     project_cot(1)
-    forward_heads(1)
+    values_grad(1)
 
     major, minor = (x, y), (y, x)
     at_major, at_minor = (at_x, at_y), (at_y, at_x)
     chunk_at = (0, 1024, 1536)
     chunk_rows = (256, 128, 128)
 
-    def columns(block):
-        lanes = slice(256 * block, 256 * block + 256)
+    def columns(lanes):
         return mm(nrmt[0], gnat[0, :, lanes]) + mm(nrmt[1], gnat[1, :, lanes])
 
     def scatter_pay(e):
@@ -359,7 +364,7 @@
                     RS1 + e, R_RS1 + e, at_major[p](to),
                 )
 
-    out = columns(2)
+    out = columns(slice(512, 768))
     for p in range(2):
         pay[p, 0:512, :] = out[:, 128 * p:128 * p + 128].astype(BF16)
     out = mm(attt[0], cotf[0]) + mm(attt[1], cotf[1])
@@ -368,18 +373,16 @@
             lanes = slice(256 * p + 128 * u, 256 * p + 128 * u + 128)
             pay[p, 512 + 256 * u:768 + 256 * u, :] = out[:, lanes].astype(BF16)
     scatter_pay(0)
-    backward_heads(0)
-    backward_heads(1)
-    out = columns(1)
-    for p in range(2):
-        pay[p, 1024:1536, :] = out[:, 128 * p:128 * p + 128].astype(BF16)
-    scatter_pay(1)
     for w in range(2):
-        gnat[w, :, 0:256] = gradt[w].T
-    out = columns(0)
-    for p in range(2):
-        pay[p, 1536:2048, :] = out[:, 128 * p:128 * p + 128].astype(BF16)
-    scatter_pay(2)
+        backward_rest(w)
+    for group in range(2):
+        for w in range(2):
+            backward_group(w, group)
+        rows = slice(1024 + 512 * group, 1536 + 512 * group)
+        out = columns(slice(256 * group, 256 * group + 256))
+        for p in range(2):
+            pay[p, rows, :] = out[:, 128 * p:128 * p + 128].astype(BF16)
+        scatter_pay(1 + group)
 
     gn_send[...] = mm(gnat[1], wqt[...])
     send(gn_send, gn_recv, PAIR + 3, PAIR + 3, sibling)
@@ -422,35 +425,6 @@
     grad_normed = grad_normed + gn_recv[...]
     standard = std[...]
     grad_gain = jnp.sum(grad_normed * standard, axis=0, keepdims=True)
-    grad_hat = grad_normed * gain_ref[...]
-    grad_in = istd[...] * (
-        grad_hat
-        - jnp.mean(grad_hat, axis=-1, keepdims=True)
-        - standard * jnp.mean(grad_hat * standard, axis=-1, keepdims=True)
-    )
-    back_send[...] = grad_in.astype(BF16).reshape(6, 12, 2, FEAT)
-    returns = (
-        ((3, 6), (0, 0), (east, north)),
-        ((0, 6), (3, 0), (east, lat)),
-        ((3, 0), (0, 6), (lon, north)),
-    )
-    for source, target, device in returns:
-        send(
-            back_send.at[pl.ds(source[0], 3), pl.ds(source[1], 6)],
-            back_recv.at[pl.ds(target[0], 3), pl.ds(target[1], 6)],
-            BACK, R_BACK, device,
-        )
-    ginf[...] = grad_in.reshape(6, 12, 2, FEAT)
-
-    for p in range(2):
-        arrived(r2.at[p], R_RS2 + p)
-        value = s1[p, span(128 * minor[p], 128), :].astype(F32)
-        for d in range(3):
-            value = value + r2[p, d].astype(F32)
-        s2[p] = value.astype(BF16)
-    for d in RING8:
-        to = (z + d) % 8
-        send(s2.at[:, span(16 * to, 16)], r3.at[d - 1], RS3, R_RS3, at_z(to))
 
     turned_rest = ds_rest[...].T
     turned = total
@@ -474,6 +448,45 @@
         to = (x + d) % 4
         send(tb.at[span(16 * to, 16)], rt1.at[d - 1], TX, R_TX, at_x(to))
 
+    for p in range(2):
+        arrived(r2.at[p], R_RS2 + p)
+        value = s1[p, span(128 * minor[p], 128), :].astype(F32)
+        for d in range(3):
+            value = value + r2[p, d].astype(F32)
+        s2[p] = value.astype(BF16)
+    for d in RING8:
+        to = (z + d) % 8
+        send(s2.at[:, span(16 * to, 16)], r3.at[d - 1], RS3, R_RS3, at_z(to))
+
+    grad_hat = grad_normed * gain_ref[...]
+    grad_in = istd[...] * (
+        grad_hat
+        - jnp.mean(grad_hat, axis=-1, keepdims=True)
+        - standard * jnp.mean(grad_hat * standard, axis=-1, keepdims=True)
+    )
+    back_send[...] = grad_in.astype(BF16).reshape(6, 12, 2, FEAT)
+    ginf[...] = grad_in.reshape(6, 12, 2, FEAT)
+
+    returns = (
+        ((3, 6), (0, 0), (east, north)),
+        ((0, 6), (3, 0), (east, lat)),
+        ((3, 0), (0, 6), (lon, north)),
+    )
+    for source, target, device in returns:
+        send(
+            back_send.at[pl.ds(source[0], 3), pl.ds(source[1], 6)],
+            back_recv.at[pl.ds(target[0], 3), pl.ds(target[1], 6)],
+            BACK, R_BACK, device,
+        )
+
+    arrived(rt1, R_TX)
+    value = tb[span(16 * x, 16), :]
+    for d in range(3):
+        value = value + rt1[d]
+    t2[...] = value
+    for d in RING4:
+        send(t2, rt2.at[d - 1], TY, R_TY, at_y((y + d) % 4))
+
     arrived(r3, R_RS3)
     for p in range(2):
         value = s2[p, span(16 * z, 16), :].astype(F32)
@@ -484,25 +497,24 @@
     for d in RING8:
         send(mine_z, mine_z, AG1, R_AG1, at_z((z + d) % 8))
 
-    arrived(rt1, R_TX)
-    value = tb[span(16 * x, 16), :]
+    arrived(rt2, R_TY)
+    value = t2[...]
     for d in range(3):
-        value = value + rt1[d]
-    t2[...] = value
-    for d in RING4:
-        send(t2, rt2.at[d - 1], TY, R_TY, at_y((y + d) % 4))
+        value = value + rt2[d]
+    t3[...] = value
+    for d in RING8:
+        send(t3, rt3.at[d - 1], TZ, R_TZ, at_z((z + d) % 8))
 
     base1 = [512 * major[p] for p in range(2)]
     base2 = [base1[p] + 128 * minor[p] for p in range(2)]
     arrived(pay.at[0, pl.ds(0, 224)], R_AG1)
     into2 = {1: R_AG2, 3: R_AG2 + 1, 2: R_AG2 + 2}
-    into3 = {1: [R_AG3] * 4, 3: [R_AG3 + 1] * 4, 2: [R_AG3 + 2, R_AG3 + 3, R_AG3 + 4, R_AG3 + 5]}
 
     def spread_major(p, e):
         rows = span(base1[p] + 128 * ((minor[p] + 4 - e) % 4), 128)
         part = big_ref.at[core, p, rows]
         for d in RING4:
-            send(g1.at[p] if e == 0 else part, part, AG3, into3[d][e], at_major[p]((major[p] + d) % 4))
+            send(g1.at[p] if e == 0 else part, part, AG3, R_AG3 + e, at_major[p]((major[p] + d) % 4))
 
     for d in RING4:
         for p in range(2):
@@ -511,31 +523,6 @@
         spread_major(p, 0)
     for p in range(2):
         big_ref[core, p, span(base2[p], 128), :] = g1[p]
-
-    arrived(rt2, R_TY)
-    value = t2[...]
-    for d in range(3):
-        value = value + rt2[d]
-    t3[...] = value
-    for d in RING8:
-        send(t3, rt3.at[d - 1], TZ, R_TZ, at_z((z + d) % 8))
-
-    def forward(p, row, count):
-        part = big_ref.at[core, p, span(row, count)]
-        send(part, part, SIB, R_SIB, sibling)
-
-    for e in (1, 3, 2):
-        arrived(g1, into2[e])
-        for p in range(2):
-            spread_major(p, e)
-    for p in range(2):
-        forward(p, base1[p], 512)
-
-    arrived(back_recv.at[:, three], R_BACK)
-    gin_ref[0:3, 0:6] = back_recv[0:3, 0:6].astype(F32)
-    gin_ref[0:3, 6:12] = back_recv[0:3, 6:12].astype(F32)
-    gin_ref[3:6, 0:6] = back_recv[3:6, 0:6].astype(F32)
-    gin_ref[3:6, 6:12] = ginf[0:3, 0:6]
 
     arrived(rt3, R_TZ)
     value = t3[...]
@@ -545,6 +532,26 @@
     mine_t[...] = value * GRAD_SCALE
     for d in RING4:
         send(mine_t, mine_t, TXG, R_TXG, at_x((x + d) % 4))
+
+    def forward(p, row, count):
+        part = big_ref.at[core, p, span(row, count)]
+        send(part, part, SIB, R_SIB, sibling)
+
+    for e in (1, 3, 2):
+        arrived(g1, into2[e])
+        for p in range(2):
+            spread_major(p, e)
+    for p in range(2):
+        forward(p, base1[p], 512)
+
+    arrived(rt1, R_TXG)
+    send(tf, tf_recv, TSIB, R_TSIB, sibling)
+
+    arrived(back_recv.at[:, three], R_BACK)
+    gin_ref[0:3, 0:6] = back_recv[0:3, 0:6].astype(F32)
+    gin_ref[0:3, 6:12] = back_recv[0:3, 6:12].astype(F32)
+    gin_ref[3:6, 0:6] = back_recv[3:6, 0:6].astype(F32)
+    gin_ref[3:6, 6:12] = ginf[0:3, 0:6]
 
     left(xw.at[:, three], XS)
     left(cw.at[:, three], COTS)
@@ -564,17 +571,11 @@
     left(rt3, TZ)
     left(back_recv.at[:, three], BACK)
 
-    for d in (1, 3):
-        arrived(pay.at[0, pl.ds(0, 1024)], into3[d][0])
-        for p in range(2):
-            forward(p, 512 * ((major[p] + 4 - d) % 4), 512)
-        if d == 1:
-            arrived(rt1, R_TXG)
-            send(tf, tf_recv, TSIB, R_TSIB, sibling)
     for e in (0, 1, 3, 2):
-        arrived(g1, into3[2][e])
-        for p in range(2):
-            forward(p, 512 * ((major[p] + 2) % 4) + 128 * ((minor[p] + 4 - e) % 4), 128)
+        arrived(pay.at[0, pl.ds(0, 768)], R_AG3 + e)
+        for d in (1, 3, 2):
+            for p in range(2):
+                forward(p, 512 * ((major[p] + 4 - d) % 4) + 128 * ((minor[p] + 4 - e) % 4), 128)
     left(pay.at[0, pl.ds(0, 768)], AG2)
     left(pay.at[:, pl.ds(0, 1536)], AG3)
     left(rt1, TXG)
@@ -604,11 +605,14 @@
     for step in range(4):
         rows = slice(128 * step, 128 * step + 128)
         for block in range(3):
-            start = (512 * step + 384, 512 * step + 256, 512 * (step // 2) + 128 * (step % 2))[block]
             for core in range(2):
                 for p in range(2):
                     lanes = slice(512 * block + 256 * core + 128 * p, 512 * block + 256 * core + 128 * p + 128)
-                    wqkv[rows, lanes] = big[core, p, start:start + 128, :].astype(F32) * GRAD_SCALE
+                    if block == 2:
+                        column, start = p, 512 * (step // 2) + 128 * (step % 2)
+                    else:
+                        column, start = 1 - block, 512 * step + 256 + 128 * p
+                    wqkv[rows, lanes] = big[core, column, start:start + 128, :].astype(F32) * GRAD_SCALE
         one = pltpu.make_async_copy(wqkv.at[pl.ds(128 * step, 128)], wqkv_out.at[pl.ds(128 * step, 128)], sem.at[3 + step])
         one.start()
         made.append(one)
@@ -675,7 +679,8 @@
             pltpu.VMEM((2, WT, 768), BF16),
             pltpu.VMEM((2, 8, WT, 128), F32),
             pltpu.VMEM((2, WT, 128), F32),
-            pltpu.VMEM((WT, 256), F32),
+            pltpu.VMEM((2, WT, 256), F32),
+            pltpu.VMEM((2, 2, WT, 512), BF16),
             pltpu.VMEM((8, WT, 128), F32),
             pltpu.VMEM((256, 128), F32),
             pltpu.VMEM((WT, FEAT), F32),

time: 58.6 us -> 57.5 us (0.981)
  Pallas kernels: 57.9 us -> 56.8 us
    pallas_call x1, Pallas kernels: 55.7 us -> 54.6 us  [per_device(): pl.pallas_call(body, out_shape=(jax.ShapeDtypeStruct((2, 2, 2048, 128), B...]
where the time goes in v5:
time: 57.5 us
  Pallas kernels  56.8 us (99%)
  between operations  0.64 us (1%)
    pallas_call x1, Pallas kernels, per_device(): pl.pallas_call(body, out_shape=(jax.ShapeDtypeStruct((2, 2, 2048, 128), B...  54.6 us
    pallas_call x1, Pallas kernels, per_device(): pl.pallas_call(widen, out_shape=(jax.ShapeDtypeStruct((6, 12, 2, FEAT), F...  2.21 us

profile of v5, /device:TPU:1, one launch (start us, length us, event | category | flops | bytes accessed | tf_op | source)
XLA Modules:
  0.0 57.5 jit_solution(12681354937964021066)
XLA Ops:
  0.6 54.6 %shard_map.119 = (bf16[2,2,2048,128]{3,2,1,0:T(8,128)(2,1)S(1)}, f32[6,12,2,512]{3,2,1,0:T(2,128)S(1)}, f32[16,759]{1,0:T(8,128)S(1)}, f32[1,512]{1,0:T(1,128)S(1)}) custom-call(bf16[6,12,2,512]{3,2,1,0:T(2,128)(2,1)} %bitcast.7, bf16[6,12,2,512]{3,2,1,0:T(2,128)(2,1)} %bitcast.8, s32[6,12]{1,0:T(8,128)} %pad_hbm.1, s32[144,144]{1,0:T(8,128)} %rel_hbm.1, ...), custom_call_target="tpu_custom_call" | custom-call | tf_op jit(solution)/shard_map/pallas_call | solution.py:635
  55.2 2.2 %shard_map.120 = (f32[6,12,2,512]{3,2,1,0:T(2,128)}, f32[1,512]{1,0:T(1,128)}, f32[512,1536]{1,0:T(8,128)}, f32[512,512]{1,0:T(8,128)}, f32[16,759]{1,0:T(8,128)}) custom-call(bf16[2,2,2048,128]{3,2,1,0:T(8,128)(2,1)S(1)} %get-tuple-element.14.big, f32[6,12,2,512]{3,2,1,0:T(2,128)S(1)} %get-tuple-element.15.gin, f32[16,759]{1,0:T(8,128)S(1)} %get-tuple-element.16.table, ...), custom_call_target="tpu_custom_call" | custom-call | tf_op jit(solution)/shard_map/pallas_call | solution.py:728

commit v6 on v5

--- a/solution.py
+++ b/solution.py
@@ -86,6 +86,14 @@
 
     def span(start, count):
         return pl.ds(pl.multiple_of(start, 16), count)
+
+    barrier = pltpu.get_barrier_semaphore()
+    partners = [at_z((z + d) % 8) for d in RING8]
+    partners += [(west, south), (east, north), (west, lat), (east, lat)]
+    partners += [at_x((x + d) % 4) for d in RING4] + [at_y((y + d) % 4) for d in RING4]
+    partners += [(lon, south), (lon, north), sibling]
+    for device in partners:
+        pl.semaphore_signal(barrier, inc=1, device_id=device, device_id_type=MESH)
 
     loads = {}
     heads_at = 256 * core
@@ -105,13 +113,6 @@
         loads[name] = pltpu.make_async_copy(src, dst, lsem.at[n])
         loads[name].start()
 
-    barrier = pltpu.get_barrier_semaphore()
-    partners = [sibling, (west, lat), (lon, south), (west, south), (east, lat), (lon, north), (east, north)]
-    partners += [at_x((x + d) % 4) for d in RING4]
-    partners += [at_y((y + d) % 4) for d in RING4]
-    partners += [at_z((z + d) % 8) for d in RING8]
-    for device in partners:
-        pl.semaphore_signal(barrier, inc=1, device_id=device, device_id_type=MESH)
     pl.semaphore_wait(barrier, len(partners))
 
     places = (
@@ -132,7 +133,6 @@
     send_quarters(x_ref, xw, XS)
     for n, (unused, unused, device) in enumerate(places):
         send(pad_hbm, pads.at[n], PADS + n, PADS + n, device)
-    send_quarters(cot_ref, cw, COTS)
 
     for name in ("rel", "bias"):
         loads[name].wait()
@@ -172,7 +172,9 @@
         gather_heads(relt[rows, :], put)
         return carry
 
-    lax.fori_loop(0, WT // 8, lookup, 0)
+    lax.fori_loop(0, 9, lookup, 0)
+    send_quarters(cot_ref, cw, COTS)
+    lax.fori_loop(9, WT // 8, lookup, 0)
     def lookup_rest(step, carry):
         part, half = step // 2, pl.ds(pl.multiple_of(8 * (step % 2), 8), 8)
 

time: 57.5 us -> 57.5 us (level)
  no operation moved by 1% of the time
where the time goes in v6:
time: 57.5 us; the launch traced here: 57.4 us
  Pallas kernels  56.7 us (99%)
  between operations  0.64 us (1%)
    pallas_call x1, Pallas kernels, per_device(): pl.pallas_call(body, out_shape=(jax.ShapeDtypeStruct((2, 2, 2048, 128), B...  54.5 us
    pallas_call x1, Pallas kernels, per_device(): pl.pallas_call(widen, out_shape=(jax.ShapeDtypeStruct((6, 12, 2, FEAT), F...  2.21 us

profile of v6, /device:TPU:1, one launch (start us, length us, event | category | flops | bytes accessed | tf_op | source)
XLA Modules:
  0.0 57.4 jit_solution(1898091094263996314)
XLA Ops:
  0.6 54.5 %shard_map.119 = (bf16[2,2,2048,128]{3,2,1,0:T(8,128)(2,1)S(1)}, f32[6,12,2,512]{3,2,1,0:T(2,128)S(1)}, f32[16,759]{1,0:T(8,128)S(1)}, f32[1,512]{1,0:T(1,128)S(1)}) custom-call(bf16[6,12,2,512]{3,2,1,0:T(2,128)(2,1)} %bitcast.7, bf16[6,12,2,512]{3,2,1,0:T(2,128)(2,1)} %bitcast.8, s32[6,12]{1,0:T(8,128)} %pad_hbm.1, s32[144,144]{1,0:T(8,128)} %rel_hbm.1, ...), custom_call_target="tpu_custom_call" | custom-call | tf_op jit(solution)/shard_map/pallas_call | solution.py:637
  55.2 2.2 %shard_map.120 = (f32[6,12,2,512]{3,2,1,0:T(2,128)}, f32[1,512]{1,0:T(1,128)}, f32[512,1536]{1,0:T(8,128)}, f32[512,512]{1,0:T(8,128)}, f32[16,759]{1,0:T(8,128)}) custom-call(bf16[2,2,2048,128]{3,2,1,0:T(8,128)(2,1)S(1)} %get-tuple-element.14.big, f32[6,12,2,512]{3,2,1,0:T(2,128)S(1)} %get-tuple-element.15.gin, f32[16,759]{1,0:T(8,128)S(1)} %get-tuple-element.16.table, ...), custom_call_target="tpu_custom_call" | custom-call | tf_op jit(solution)/shard_map/pallas_call | solution.py:730
